TPU v7x, 512 devices: a whole 4x8x8 slice. The times are simulated.
512 devices in a mesh: lat: 32 (over x_hi, z, core), lon: 16 (over x_lo, y).
Axes of the slice: x: 4 (x_hi: 2, x_lo: 2; x = x_hi * 2 + x_lo), y: 8, z: 8, core: 2. Of those that a mesh axis runs over, the one named last changes fastest.
Arguments:
- winds: float32 [2, 288, 46080], P(None, 'lat', 'lon'), as said below
- thickness: float32 [288, 46080], P('lat', 'lon'), may hold values from 0.5 to 1.5
- tracers: bfloat16 [3, 288, 46080], P(None, 'lat', 'lon'), may hold values from 0 to 1
- cutoff: int32 [288], replicated, may hold values from 1 to 1440, as said below
Outputs:
- new_winds: float32 [2, 288, 46080], P(None, 'lat', 'lon')
- new_thickness: float32 [288, 46080], P('lat', 'lon')
- tracer_mass: bfloat16 [3, 288, 46080], P(None, 'lat', 'lon')
Inputs may be any that keep to these rules, and one draw needn't show every extreme that they name: `cutoff`: the 48 rows nearest each pole have cutoffs that grow from 1 at the pole row to at most a quarter of 2880; every other row has exactly 1440, so that the filter leaves it unchanged. `winds`: each wind is the cosine of its row's latitude times a value of order one.
All inputs are finite; a program needn't handle non-finite values.
Results may differ from a plain program's by a relative error of at most 0.001.
Values sent between devices are 32-bit elements; how exact they have to be, the bound alone decides.
A program may use at most 64 MiB of HBM per device.

v0:
```python
import functools
import math

import jax
import jax.numpy as jnp
import numpy as np
from jax import lax
from jax.experimental import pallas as pl
from jax.experimental.pallas import tpu as pltpu
from jax.sharding import PartitionSpec as P

MESH = pl.DeviceIdType.MESH
F32 = jnp.float32
BF16 = jnp.bfloat16

LEVELS = 16
NLAT = 288
NLON = 2880
POLAR = 48
TIME_STEP = 0.05
DIFFUSION = 0.5
RATIO = 2.0 * NLAT / NLON

N_LAT = 32
N_LON = 16
ROWS = NLAT // N_LAT
COLS = NLON // N_LON
WIDE = COLS * LEVELS

LANES = 128
PER = LANES // LEVELS
TILES = 24
FULL = WIDE // LANES
TAIL = WIDE - FULL * LANES
FIELDS = 6
SLOT = FIELDS * TILES
EDGE = 5 * TILES
PAIRS = 3 * ROWS
BLOCK = TILES
OWN = N_LON
AWAY = PAIRS - OWN

BASE = NLON // PER
HALF = BASE // 2 + 1
FREQ = 184
SIDE = N_LON // 2 * TILES


def geometry():
    row = np.arange(NLAT, dtype=np.float64)
    centre = (row + 0.5) * (math.pi / NLAT) - math.pi / 2

    def face(index):
        inside = (index >= 0) & (index < NLAT - 1)
        return np.where(inside, np.sin((index + 1) * (math.pi / NLAT)), 0.0)

    table = np.stack([1.0 / np.cos(centre), np.sin(centre), face(row), face(row - 1)], axis=1)
    return table.astype(np.float32).reshape(-1)


def split_table(table):
    high = table.astype(np.float32).astype(jnp.bfloat16)
    low = (table - high.astype(np.float64)).astype(np.float32).astype(jnp.bfloat16)
    return np.concatenate([high, low], axis=0)


def filter_tables():
    turn = 2.0 * math.pi
    freq = np.arange(FREQ)
    live = (freq < HALF).astype(np.float64)
    sector, tile = (a.reshape(-1) for a in np.meshgrid(np.arange(N_LON // 2), np.arange(TILES), indexing="ij"))
    used = (tile * PER < COLS).astype(np.float64)
    place = 2 * COLS * sector // PER + tile
    angle = turn * ((freq[:, None] * place[None, :]) % BASE) / BASE
    weight = live[:, None] * used[None, :]
    fore = np.concatenate([np.cos(angle) * weight, -np.sin(angle) * weight], axis=0)
    twice = np.where((freq == 0) | (freq == HALF - 1), 1.0, 2.0) / NLON
    back = np.concatenate([np.cos(angle) * weight * twice[:, None], -np.sin(angle) * weight * twice[:, None]], axis=0).T

    lane = np.arange(2 * LANES)
    shift = lane % LANES // LEVELS + COLS * (lane // LANES)
    angle = turn * ((freq[:, None] * shift[None, :]) % NLON) / NLON
    twiddle = np.concatenate([np.cos(angle), np.sin(angle)], axis=0).astype(np.float32)

    out = np.arange(LANES)
    angle = turn * ((BASE * shift[:, None] * (out // LEVELS)[None, :]) % NLON) / NLON
    same = (lane % LEVELS)[:, None] == (out % LEVELS)[None, :]
    cosine, sine = np.cos(angle) * same, np.sin(angle) * same
    mix = np.concatenate(
        [np.concatenate([cosine, -sine], axis=1), np.concatenate([sine, cosine], axis=1)], axis=0
    )
    return split_table(fore), twiddle, split_table(mix), split_table(mix.T), split_table(back)


def split(value):
    high = value.astype(BF16)
    low = (value - high.astype(F32)).astype(BF16)
    return high, low


def dot(a, b):
    return jnp.dot(a, b, preferred_element_type=F32)


def table_left(table, rows, value):
    high, low = split(value)
    first = table[pl.ds(0, rows), :]
    return dot(first, high) + dot(first, low) + dot(table[pl.ds(rows, rows), :], high)


def table_right(value, table, rows):
    high, low = split(value)
    first = table[pl.ds(0, rows), :]
    return dot(high, first) + dot(low, first) + dot(high, table[pl.ds(rows, rows), :])


def eastward(value):
    lane = lax.broadcasted_iota(jnp.int32, (TILES, LANES), 1)
    here = pltpu.roll(value, LANES - LEVELS, 1)
    return jnp.where(lane < LANES - LEVELS, here, pltpu.roll(here, TILES - 1, 0))


def westward(value):
    lane = lax.broadcasted_iota(jnp.int32, (TILES, LANES), 1)
    here = pltpu.roll(value, LEVELS, 1)
    return jnp.where(lane >= LEVELS, here, pltpu.roll(here, 1, 0))


def kernel(
    cut, geo, winds_in, thick_in, mass_in, fore_in, twiddle_in, mix_in, unmix_in, back_in,
    winds_out, thick_out, mass_out,
    wv, hv, qv, mv, cells, to_east, to_west, from_west, from_east, tend, gathered, sent_back, returned, mass,
    fore, twiddle, mix, unmix, back,
    in_sem, table_sem, out_sem, halo_send, halo_recv, go_send, go_recv, back_send, back_recv,
):
    lat = lax.axis_index("lat")
    lon = lax.axis_index("lon")
    polar_south = lat * ROWS < POLAR
    polar_north = (lat + 1) * ROWS > NLAT - POLAR
    polar = jnp.logical_or(polar_south, polar_north)
    other = (lat + N_LAT // 2) % N_LAT
    other_polar = jnp.logical_or(other * ROWS < POLAR, (other + 1) * ROWS > NLAT - POLAR)
    lends = jnp.logical_and(other_polar, lon < AWAY)

    loads = [
        pltpu.make_async_copy(winds_in, wv, in_sem.at[0]),
        pltpu.make_async_copy(thick_in, hv, in_sem.at[1]),
        pltpu.make_async_copy(mass_in, qv, in_sem.at[2]),
    ]
    for load in loads:
        load.start()
    tables = [
        pltpu.make_async_copy(source, target, table_sem.at[i])
        for i, (source, target) in enumerate(
            ((fore_in, fore), (twiddle_in, twiddle), (mix_in, mix), (unmix_in, unmix), (back_in, back))
        )
    ]
    for load in tables:
        load.start()

    east = (lat, (lon + 1) % N_LON)
    west = (lat, (lon + N_LON - 1) % N_LON)
    below = (lat + N_LAT - 1) // N_LAT
    above = 1 - lat // (N_LAT - 1)
    south = (lat - below, (lon + (1 - below) * (N_LON // 2)) % N_LON)
    north = (lat + above, (lon + (1 - above) * (N_LON // 2)) % N_LON)

    barrier = pltpu.get_barrier_semaphore()

    def greet(device):
        pl.semaphore_signal(barrier, inc=1, device_id=device, device_id_type=MESH)

    for device in (east, west, south, north):
        greet(device)

    @pl.when(polar)
    def _():
        lax.fori_loop(1, N_LON, lambda i, c: (greet((lat, (lon + i) % N_LON)), c)[1], 0)
        lax.fori_loop(0, AWAY, lambda i, c: (greet((other, i)), c)[1], 0)

    @pl.when(lends)
    def _():
        lax.fori_loop(0, N_LON, lambda i, c: (greet((other, i)), c)[1], 0)

    for load in loads:
        load.wait()

    fields = (
        lambda at: hv[:, at],
        lambda at: wv[1, :, at],
        lambda at: qv[0, :, at].astype(F32),
        lambda at: qv[1, :, at].astype(F32),
        lambda at: qv[2, :, at].astype(F32),
        lambda at: wv[0, :, at],
    )

    def spread(t, carry):
        at = pl.ds(pl.multiple_of(t * LANES, LANES), LANES)
        for f, get in enumerate(fields):
            cells[pl.ds(SLOT + f * TILES + t, ROWS, stride=SLOT), :] = get(at)
        return carry

    lax.fori_loop(0, FULL, spread, 0)
    blank = jnp.zeros((ROWS, LANES - TAIL), F32)
    for f, get in enumerate(fields):
        last = jnp.concatenate([get(pl.ds(FULL * LANES, TAIL)), blank], axis=1)
        cells[pl.ds(SLOT + f * TILES + FULL, ROWS, stride=SLOT), :] = last

    sides = (0, 2, 3, 4, 5)
    for i, f in enumerate(sides):
        get = fields[f]
        to_west[pl.ds(i * ROWS, ROWS), :] = pltpu.roll(get(pl.ds(0, LANES)), TAIL, 1)
        last = jnp.concatenate([get(pl.ds(FULL * LANES, TAIL)), blank], axis=1)
        to_east[pl.ds(i * ROWS, ROWS), :] = pltpu.roll(last, LANES - TAIL, 1)

    @pl.when(polar)
    def _():
        pl.semaphore_wait(barrier, 4 + N_LON - 1 + AWAY)

    @pl.when(lends)
    def _():
        pl.semaphore_wait(barrier, 4 + N_LON)

    @pl.when(jnp.logical_not(jnp.logical_or(polar, lends)))
    def _():
        pl.semaphore_wait(barrier, 4)

    south_slot = below * (ROWS + 1)
    north_slot = (1 - above) * (ROWS + 1)

    def edge(slot):
        return cells.at[pl.ds(pl.multiple_of(slot * SLOT, 8), EDGE), :]

    halos = [
        pltpu.make_async_remote_copy(
            edge(1), edge(south_slot), halo_send.at[0], halo_recv.at[below], device_id=south, device_id_type=MESH
        ),
        pltpu.make_async_remote_copy(
            edge(ROWS), edge(north_slot), halo_send.at[1], halo_recv.at[1 - above],
            device_id=north, device_id_type=MESH,
        ),
        pltpu.make_async_remote_copy(
            to_east, from_west, halo_send.at[2], halo_recv.at[2], device_id=east, device_id_type=MESH
        ),
        pltpu.make_async_remote_copy(
            to_west, from_east, halo_send.at[3], halo_recv.at[3], device_id=west, device_id_type=MESH
        ),
    ]
    for halo in halos:
        halo.start()
    pltpu.make_async_copy(edge(0), edge(0), halo_recv.at[0]).wait()
    pltpu.make_async_copy(edge(ROWS + 1), edge(ROWS + 1), halo_recv.at[1]).wait()
    pltpu.make_async_copy(from_west, from_west, halo_recv.at[2]).wait()
    pltpu.make_async_copy(from_east, from_east, halo_recv.at[3]).wait()
    halos[0].wait_send()
    halos[1].wait_send()

    lane = lax.broadcasted_iota(jnp.int32, (ROWS, LANES), 1)
    for i, f in enumerate(sides):
        at = pl.ds(SLOT + f * TILES + FULL, ROWS, stride=SLOT)
        here = from_east[pl.ds(i * ROWS, ROWS), :]
        cells[at, :] = jnp.where((lane >= TAIL) & (lane < TAIL + LEVELS), here, cells[at, :])
        at = pl.ds(SLOT + f * TILES + FULL + 1, ROWS, stride=SLOT)
        here = from_west[pl.ds(i * ROWS, ROWS), :]
        cells[at, :] = jnp.where(lane >= LANES - LEVELS, here, 0.0)

    @pl.when(lat == 0)
    def _():
        cells[pl.ds(TILES, TILES), :] = -cells[pl.ds(TILES, TILES), :]

    @pl.when(lat == N_LAT - 1)
    def _():
        at = pl.ds((ROWS + 1) * SLOT + TILES, TILES)
        cells[at, :] = -cells[at, :]

    def row(slot, field):
        return cells[pl.ds(pl.multiple_of(slot * SLOT + field * TILES, 8), TILES), :]

    def scalars(j):
        at = (lat * ROWS + j) * 4
        return geo[at], geo[at + 1], geo[at + 2], geo[at + 3]

    flat = lax.broadcasted_iota(jnp.int32, (TILES, LANES), 0) * LANES + lax.broadcasted_iota(
        jnp.int32, (TILES, LANES), 1
    )
    valid = flat < WIDE

    def fluxes(j, cos_north, cos_south):
        h, h_n, h_s = row(j + 1, 0), row(j + 2, 0), row(j, 0)
        v, v_n, v_s = row(j + 1, 1), row(j + 2, 1), row(j, 1)
        u = row(j + 1, 5)
        h_e, h_w = eastward(h), westward(h)
        flux_e = 0.5 * (u + eastward(u)) * (0.5 * (h + h_e))
        flux_w = 0.5 * (westward(u) + u) * (0.5 * (h_w + h))
        flux_n = 0.5 * (v + v_n) * (0.5 * (h + h_n)) * cos_north
        flux_s = 0.5 * (v_s + v) * (0.5 * (h_s + h)) * cos_south
        return h, u, v, h_e, h_w, h_n, h_s, flux_e, flux_w, flux_n, flux_s

    def tendency(j, carry):
        inverse, sine, cos_north, cos_south = scalars(j)
        h, u, v, h_e, h_w, h_n, h_s, flux_e, flux_w, flux_n, flux_s = fluxes(j, cos_north, cos_south)
        values = (
            -((flux_e - flux_w) + RATIO * (flux_n - flux_s)) * inverse,
            sine * v - (h_e - h_w) * (0.5 * inverse),
            -sine * u - RATIO * (h_n - h_s) * 0.5,
        )
        for f, value in enumerate(values):
            at = pl.ds(pl.multiple_of((j * 3 + f) * BLOCK, 8), BLOCK)
            tend[at, :] = jnp.where(valid, value, 0.0)
        return carry

    lax.fori_loop(0, ROWS, tendency, 0)

    def block(ref, index):
        return ref.at[pl.ds(pl.multiple_of(index * BLOCK, 8), BLOCK), :]

    def place(sector):
        return (sector % 2) * (N_LON // 2) + sector // 2

    def go(pair, device):
        return pltpu.make_async_remote_copy(
            block(tend, pair), block(gathered, place(lon)), go_send, go_recv, device_id=device, device_id_type=MESH
        )

    @pl.when(polar)
    def _():
        def own(i, carry):
            target = (lon + i) % N_LON
            go(target, (lat, target)).start()
            return carry

        def away(i, carry):
            target = (lon + i) % AWAY
            go(OWN + target, (other, target)).start()
            return carry

        lax.fori_loop(0, AWAY, away, 0)
        lax.fori_loop(1, N_LON, own, 0)
        at = pl.ds(pl.multiple_of(place(lon) * BLOCK, 8), BLOCK)
        gathered[at, :] = tend[pl.ds(pl.multiple_of(lon * BLOCK, 8), BLOCK), :]

    def tracer(j, carry):
        inverse, sine, cos_north, cos_south = scalars(j)
        h, u, v, h_e, h_w, h_n, h_s, flux_e, flux_w, flux_n, flux_s = fluxes(j, cos_north, cos_south)
        for c in range(3):
            q, q_n, q_s = row(j + 1, 2 + c), row(j + 2, 2 + c), row(j, 2 + c)
            q_e, q_w = eastward(q), westward(q)
            zonal = flux_e * (0.5 * (q + q_e)) - flux_w * (0.5 * (q_w + q))
            merid = flux_n * (0.5 * (q + q_n)) - flux_s * (0.5 * (q_s + q))
            flux = (zonal + RATIO * merid) * inverse
            laplace = (q_e + q_w) + (q_n + q_s) - 4.0 * q
            at = pl.ds(pl.multiple_of((c * ROWS + j) * TILES, 8), TILES)
            mass[at, :] = h * q + TIME_STEP * (DIFFUSION * laplace - flux)
        return carry

    lax.fori_loop(0, ROWS, tracer, 0)

    def narrow(t, carry):
        at = pl.ds(pl.multiple_of(t * LANES, LANES), LANES)
        for c in range(3):
            mv[c, :, at] = mass[pl.ds(c * ROWS * TILES + t, ROWS, stride=TILES), :].astype(BF16)
        return carry

    lax.fori_loop(0, FULL, narrow, 0)
    for c in range(3):
        last = mass[pl.ds(c * ROWS * TILES + FULL, ROWS, stride=TILES), :]
        mv[c, :, pl.ds(FULL * LANES, TAIL)] = last[:, :TAIL].astype(BF16)
    stores = [pltpu.make_async_copy(mv, mass_out, out_sem.at[0])]
    stores[0].start()

    for load in tables:
        load.wait()

    def circle(pair_row):
        cutoff = cut[pair_row]
        data = jnp.concatenate([gathered[pl.ds(0, SIDE), :], gathered[pl.ds(SIDE, SIDE), :]], axis=1)
        lines = table_left(fore, 2 * FREQ, data)
        real, imag = lines[:FREQ], lines[FREQ:]
        cosine, sine = twiddle[pl.ds(0, FREQ), :], twiddle[pl.ds(FREQ, FREQ), :]
        turned = jnp.concatenate([real * cosine + imag * sine, imag * cosine - real * sine], axis=1)
        spectrum = table_right(turned, mix, 4 * LANES)
        wave = lax.broadcasted_iota(jnp.int32, (FREQ, 2 * LANES), 0) + BASE * (
            lax.broadcasted_iota(jnp.int32, (FREQ, 2 * LANES), 1) % LANES // LEVELS
        )
        wave = jnp.minimum(wave, NLON - wave)
        spectrum = jnp.where(wave <= cutoff, spectrum, 0.0)
        lines = table_right(spectrum, unmix, 2 * LANES)
        real, imag = lines[:, : 2 * LANES], lines[:, 2 * LANES :]
        turned = jnp.concatenate([real * cosine - imag * sine, real * sine + imag * cosine], axis=0)
        result = table_left(back, SIDE, turned)
        sent_back[pl.ds(0, SIDE), :] = result[:, :LANES]
        sent_back[pl.ds(SIDE, SIDE), :] = result[:, LANES:]

    def home(pair, sector, device):
        return pltpu.make_async_remote_copy(
            block(sent_back, place(sector)), block(returned, pair), back_send, back_recv,
            device_id=device, device_id_type=MESH,
        )

    def total(ref, blocks):
        return ref.at[pl.ds(0, blocks * BLOCK), :]

    def wait_for(ref, blocks, sem):
        pltpu.make_async_copy(total(ref, blocks), total(ref, blocks), sem).wait()

    @pl.when(polar)
    def _():
        wait_for(gathered, N_LON - 1, go_recv)
        circle(lat * ROWS + lon // 3)

        def own(i, carry):
            target = (lon + i) % N_LON
            home(lon, target, (lat, target)).start()
            return carry

        lax.fori_loop(1, N_LON, own, 0)
        at = pl.ds(pl.multiple_of(place(lon) * BLOCK, 8), BLOCK)
        returned[pl.ds(pl.multiple_of(lon * BLOCK, 8), BLOCK), :] = sent_back[at, :]

    @pl.when(lends)
    def _():
        wait_for(gathered, N_LON, go_recv)
        circle(other * ROWS + (OWN + lon) // 3)

        def away(i, carry):
            target = (lon + i) % N_LON
            home(OWN + lon, target, (other, target)).start()
            return carry

        lax.fori_loop(0, N_LON, away, 0)

    def update(source):
        def whole(t, carry):
            at = pl.ds(pl.multiple_of(t * LANES, LANES), LANES)
            step = [source[pl.ds(f * TILES + t, ROWS, stride=3 * TILES), :] for f in range(3)]
            hv[:, at] = hv[:, at] + TIME_STEP * step[0]
            wv[0, :, at] = wv[0, :, at] + TIME_STEP * step[1]
            wv[1, :, at] = wv[1, :, at] + TIME_STEP * step[2]
            return carry

        lax.fori_loop(0, FULL, whole, 0)
        at = pl.ds(FULL * LANES, TAIL)
        step = [source[pl.ds(f * TILES + FULL, ROWS, stride=3 * TILES), :][:, :TAIL] for f in range(3)]
        hv[:, at] = hv[:, at] + TIME_STEP * step[0]
        wv[0, :, at] = wv[0, :, at] + TIME_STEP * step[1]
        wv[1, :, at] = wv[1, :, at] + TIME_STEP * step[2]

    @pl.when(polar)
    def _():
        wait_for(returned, PAIRS - 1, back_recv)
        update(returned)

    @pl.when(jnp.logical_not(polar))
    def _():
        update(tend)

    stores += [
        pltpu.make_async_copy(wv, winds_out, out_sem.at[1]),
        pltpu.make_async_copy(hv, thick_out, out_sem.at[2]),
    ]
    stores[1].start()
    stores[2].start()
    halos[2].wait_send()
    halos[3].wait_send()

    @pl.when(polar)
    def _():
        wait_for(tend, PAIRS - 1, go_send)
        wait_for(sent_back, N_LON - 1, back_send)

    @pl.when(lends)
    def _():
        wait_for(sent_back, N_LON, back_send)

    for store in stores:
        store.wait()


def local(winds, thickness, tracers, cutoff):
    fore, twiddle, mix, unmix, back = filter_tables()
    anywhere = pl.BlockSpec(memory_space=pl.ANY)
    scalar = pl.BlockSpec(memory_space=pltpu.SMEM)
    side = pltpu.VMEM((48, LANES), F32)
    dma = pltpu.SemaphoreType.DMA
    return pl.pallas_call(
        kernel,
        out_shape=(
            jax.ShapeDtypeStruct((2, ROWS, WIDE), F32),
            jax.ShapeDtypeStruct((ROWS, WIDE), F32),
            jax.ShapeDtypeStruct((3, ROWS, WIDE), BF16),
        ),
        in_specs=[scalar, scalar] + [anywhere] * 8,
        out_specs=(anywhere,) * 3,
        scratch_shapes=[
            pltpu.VMEM((2, ROWS, WIDE), F32),
            pltpu.VMEM((ROWS, WIDE), F32),
            pltpu.VMEM((3, ROWS, WIDE), BF16),
            pltpu.VMEM((3, ROWS, WIDE), BF16),
            pltpu.VMEM(((ROWS + 2) * SLOT, LANES), F32),
            side, side, side, side,
            pltpu.VMEM((PAIRS * BLOCK, LANES), F32),
            pltpu.VMEM((N_LON * BLOCK, LANES), F32),
            pltpu.VMEM((N_LON * BLOCK, LANES), F32),
            pltpu.VMEM((PAIRS * BLOCK, LANES), F32),
            pltpu.VMEM((PAIRS * BLOCK, LANES), F32),
            pltpu.VMEM(fore.shape, BF16),
            pltpu.VMEM(twiddle.shape, F32),
            pltpu.VMEM(mix.shape, BF16),
            pltpu.VMEM(unmix.shape, BF16),
            pltpu.VMEM(back.shape, BF16),
            dma((3,)), dma((5,)), dma((3,)), dma((4,)), dma((4,)), dma, dma, dma, dma,
        ],
        compiler_params=pltpu.CompilerParams(
            collective_id=0, has_side_effects=True, vmem_limit_bytes=40 * 1024 * 1024
        ),
        name="substep",
    )(cutoff, geometry(), winds, thickness, tracers, fore, twiddle, mix, unmix, back)


def solution(mesh):
    in_specs = (P(None, "lat", "lon"), P("lat", "lon"), P(None, "lat", "lon"), P())
    out_specs = (P(None, "lat", "lon"), P("lat", "lon"), P(None, "lat", "lon"))
    return jax.shard_map(local, mesh=mesh, in_specs=in_specs, out_specs=out_specs, check_vma=False)
```

profile of v0, /device:TPU:1, one launch (start us, length us, event | category | flops | bytes accessed | tf_op | source)
XLA Modules:
  0.0 44.1 jit_solution(5492234158867618843)
XLA Ops:
  0.6 0.0 copy-start
  0.6 0.0 copy-start.1
  0.7 1.0 %copy.14.mass_in = bf16[3,9,2880]{2,1,0:T(8,128)(2,1)S(1)} copy(bf16[3,9,2880]{2,0,1:T(4,128)(2,1)} %param.12) | data formatting | bytes 311040 | tf_op args[2]
  1.7 0.0 copy-start.6
  1.7 0.0 copy-start.7
  1.7 1.0 %copy.13.winds_in = f32[2,9,2880]{2,1,0:T(8,128)S(1)} copy(f32[2,9,2880]{2,0,1:T(2,128)} %param.10) | data formatting | bytes 414720 | tf_op args[0]
  2.7 0.0 copy-done
  2.7 0.0 copy-done.1
  2.7 0.0 copy-done.6
  2.7 0.0 copy-done.7
  2.7 0.0 copy-start.2
  2.8 1.0 %copy-done.2 = f32[368,256]{1,0:T(8,128)S(1)} copy-done((f32[368,256]{1,0:T(8,128)S(1)}, f32[368,256]{1,0:T(8,128)}, u32[]{:S(2)}) %copy-start.2) | copy-done | bytes 376856
  3.7 0.0 copy-start.3
  3.7 1.0 %copy-done.3 = bf16[736,192]{1,0:T(8,128)(2,1)S(1)} copy-done((bf16[736,192]{1,0:T(8,128)(2,1)S(1)}, bf16[736,192]{1,0:T(8,128)(2,1)}, u32[]{:S(2)}) %copy-start.3) | copy-done | bytes 282648
  4.7 0.0 copy-start.4
  4.7 1.0 %copy-done.4 = bf16[384,368]{1,0:T(8,128)(2,1)S(1)} copy-done((bf16[384,368]{1,0:T(8,128)(2,1)S(1)}, bf16[384,368]{1,0:T(8,128)(2,1)}, u32[]{:S(2)}) %copy-start.4) | copy-done | bytes 282648
  5.7 0.0 copy-start.5
  5.7 0.9 %copy-done.5 = f32[9,2880]{1,0:T(8,128)S(1)} copy-done((f32[9,2880]{1,0:T(8,128)S(1)}, f32[9,2880]{1,0:T(8,128)}, u32[]{:S(2)}) %copy-start.5) | copy-done | bytes 103704
  6.6 35.3 %substep.1 = (f32[2,9,2880]{2,1,0:T(8,128)S(1)}, f32[9,2880]{1,0:T(8,128)S(1)}, bf16[3,9,2880]{2,1,0:T(8,128)(2,1)S(1)}) custom-call(s32[288]{0:T(512)S(1)} %copy-done.7, f32[1152]{0:T(1024)S(1)} %copy-done.6, f32[2,9,2880]{2,1,0:T(8,128)S(1)} %copy.13.winds_in, f32[9,2880]{1,0:T(8,128)S(1)} %copy-done.5, bf16[3,9,2880]{2,1,0:T(8,128)(2,1)S(1)} %copy.14.mass_in, ...), custom_call_target="tpu_custom_call" | custom-call | tf_op jit(solution)/shard_map/substep/pallas_call | solution.py:485
  41.9 0.8 %copy.15 = f32[2,9,2880]{2,0,1:T(2,128)} copy(f32[2,9,2880]{2,1,0:T(8,128)S(1)} %get-tuple-element.3) | data formatting | bytes 414720 | tf_op jit(solution)/shard_map/substep/pallas_call | solution.py:485
  42.7 0.8 %copy.16 = bf16[3,9,2880]{2,0,1:T(4,128)(2,1)} copy(bf16[3,9,2880]{2,1,0:T(8,128)(2,1)S(1)} %get-tuple-element.5) | data formatting | bytes 311040 | tf_op jit(solution)/shard_map/substep/pallas_call | solution.py:485
  43.5 0.7 %copy.18 = f32[9,2880]{1,0:T(8,128)} copy(f32[9,2880]{1,0:T(8,128)S(1)} %get-tuple-element.10) | data formatting | bytes 207360
Async XLA Ops:
  0.6 2.1 %copy-start = (bf16[512,512]{1,0:T(8,128)(2,1)S(1)}, bf16[512,512]{1,0:T(8,128)(2,1)}, u32[]{:S(2)}) copy-start(bf16[512,512]{1,0:T(8,128)(2,1)} %constant.16.clone.unmix_in) | copy-start | bytes 1572868
  0.6 2.1 %copy-start.1 = (bf16[1024,256]{1,0:T(8,128)(2,1)S(1)}, bf16[1024,256]{1,0:T(8,128)(2,1)}, u32[]{:S(2)}) copy-start(bf16[1024,256]{1,0:T(8,128)(2,1)} %constant.15.clone.mix_in) | copy-start | bytes 1572868
  1.7 1.0 %copy-start.6 = (f32[1152]{0:T(1024)S(1)}, f32[1152]{0:T(1024)}, u32[]{:S(2)}) copy-start(f32[1152]{0:T(1024)} %constant.12.clone.geo) | copy-start | bytes 13828
  1.7 1.0 %copy-start.7 = (s32[288]{0:T(512)S(1)}, s32[288]{0:T(512)}, u32[]{:S(2)}) copy-start(s32[288]{0:T(512)} %cut.1) | copy-start | bytes 3460
  2.7 1.0 %copy-start.2 = (f32[368,256]{1,0:T(8,128)S(1)}, f32[368,256]{1,0:T(8,128)}, u32[]{:S(2)}) copy-start(f32[368,256]{1,0:T(8,128)} %constant.14.clone.twiddle_in) | copy-start | bytes 1130500
  3.7 1.0 %copy-start.3 = (bf16[736,192]{1,0:T(8,128)(2,1)S(1)}, bf16[736,192]{1,0:T(8,128)(2,1)}, u32[]{:S(2)}) copy-start(bf16[736,192]{1,0:T(8,128)(2,1)} %constant.13.clone.fore_in) | copy-start | bytes 847876
  4.7 1.0 %copy-start.4 = (bf16[384,368]{1,0:T(8,128)(2,1)S(1)}, bf16[384,368]{1,0:T(8,128)(2,1)}, u32[]{:S(2)}) copy-start(bf16[384,368]{1,0:T(8,128)(2,1)} %constant.17.clone.back_in) | copy-start | bytes 847876
  5.7 0.9 %copy-start.5 = (f32[9,2880]{1,0:T(8,128)S(1)}, f32[9,2880]{1,0:T(8,128)}, u32[]{:S(2)}) copy-start(f32[9,2880]{1,0:T(8,128)} %thick_in.1) | copy-start | bytes 311044
where the time goes:
time: 44.4 us; the launch traced here: 44.1 us
  Pallas kernels  35.3 us (80%)
  local copies, waits for them, and re-layouts  8.14 us (18%)
  between operations  0.72 us (2%)
    pallas_call x1, Pallas kernels, local(): pl.pallas_call(kernel, out_shape=(jax.ShapeDtypeStruct((2, ROWS, WIDE), F...  35.3 us
    unnamed x19, local copies, waits for them, and re-layouts  6.58 us
    pallas_call x2, local copies, waits for them, and re-layouts, local(): pl.pallas_call(kernel, out_shape=(jax.ShapeDtypeStruct((2, ROWS, WIDE), F...  1.56 us

commit v1 on v0

--- a/solution.py
+++ b/solution.py
@@ -43,6 +43,7 @@
 BASE = NLON // PER
 HALF = BASE // 2 + 1
 FREQ = 184
+VMEM_MIB = 63
 SIDE = N_LON // 2 * TILES
 
 
@@ -128,10 +129,10 @@
 
 def kernel(
     cut, geo, winds_in, thick_in, mass_in, fore_in, twiddle_in, mix_in, unmix_in, back_in,
-    winds_out, thick_out, mass_out,
-    wv, hv, qv, mv, cells, to_east, to_west, from_west, from_east, tend, gathered, sent_back, returned, mass,
+    returned, mass,
+    wv, hv, qv, cells, to_east, to_west, from_west, from_east, tend, gathered, sent_back,
     fore, twiddle, mix, unmix, back,
-    in_sem, table_sem, out_sem, halo_send, halo_recv, go_send, go_recv, back_send, back_recv,
+    in_sem, table_sem, halo_send, halo_recv, go_send, go_recv, back_send, back_recv,
 ):
     lat = lax.axis_index("lat")
     lon = lax.axis_index("lon")
@@ -185,32 +186,30 @@
     for load in loads:
         load.wait()
 
-    fields = (
-        lambda at: hv[:, at],
-        lambda at: wv[1, :, at],
-        lambda at: qv[0, :, at].astype(F32),
-        lambda at: qv[1, :, at].astype(F32),
-        lambda at: qv[2, :, at].astype(F32),
-        lambda at: wv[0, :, at],
-    )
-
-    def spread(t, carry):
-        at = pl.ds(pl.multiple_of(t * LANES, LANES), LANES)
-        for f, get in enumerate(fields):
-            cells[pl.ds(SLOT + f * TILES + t, ROWS, stride=SLOT), :] = get(at)
+    def padded(value):
+        return jnp.concatenate([value, jnp.zeros((value.shape[0], LANES - TAIL), F32)], axis=1)
+
+    def place_row(j, carry):
+        start = (j + 1) * SLOT
+        for t in range(FULL + 1):
+            at = pl.ds(t * LANES, LANES if t < FULL else TAIL)
+            wind, ratio = wv[j, :, at], qv[j, :, at].astype(F32)
+            if t == FULL:
+                wind, ratio = padded(wind), padded(ratio)
+            cells[pl.ds(start + t, 2, stride=TILES), :] = wind
+            cells[pl.ds(start + 3 * TILES + t, 3, stride=TILES), :] = ratio
         return carry
 
-    lax.fori_loop(0, FULL, spread, 0)
-    blank = jnp.zeros((ROWS, LANES - TAIL), F32)
-    for f, get in enumerate(fields):
-        last = jnp.concatenate([get(pl.ds(FULL * LANES, TAIL)), blank], axis=1)
-        cells[pl.ds(SLOT + f * TILES + FULL, ROWS, stride=SLOT), :] = last
+    lax.fori_loop(0, ROWS, place_row, 0)
+    for t in range(FULL + 1):
+        value = hv[:, pl.ds(t * LANES, LANES if t < FULL else TAIL)]
+        cells[pl.ds(SLOT + 2 * TILES + t, ROWS, stride=SLOT), :] = value if t < FULL else padded(value)
 
     sides = (0, 2, 3, 4, 5)
     for i, f in enumerate(sides):
-        get = fields[f]
-        to_west[pl.ds(i * ROWS, ROWS), :] = pltpu.roll(get(pl.ds(0, LANES)), TAIL, 1)
-        last = jnp.concatenate([get(pl.ds(FULL * LANES, TAIL)), blank], axis=1)
+        first = cells[pl.ds(SLOT + f * TILES, ROWS, stride=SLOT), :]
+        last = cells[pl.ds(SLOT + f * TILES + FULL, ROWS, stride=SLOT), :]
+        to_west[pl.ds(i * ROWS, ROWS), :] = pltpu.roll(first, TAIL, 1)
         to_east[pl.ds(i * ROWS, ROWS), :] = pltpu.roll(last, LANES - TAIL, 1)
 
     @pl.when(polar)
@@ -229,7 +228,7 @@
     north_slot = (1 - above) * (ROWS + 1)
 
     def edge(slot):
-        return cells.at[pl.ds(pl.multiple_of(slot * SLOT, 8), EDGE), :]
+        return cells.at[pl.ds(pl.multiple_of(slot * SLOT + TILES, 8), EDGE), :]
 
     halos = [
         pltpu.make_async_remote_copy(
@@ -266,7 +265,8 @@
 
     @pl.when(lat == 0)
     def _():
-        cells[pl.ds(TILES, TILES), :] = -cells[pl.ds(TILES, TILES), :]
+        at = pl.ds(TILES, TILES)
+        cells[at, :] = -cells[at, :]
 
     @pl.when(lat == N_LAT - 1)
     def _():
@@ -286,9 +286,9 @@
     valid = flat < WIDE
 
     def fluxes(j, cos_north, cos_south):
-        h, h_n, h_s = row(j + 1, 0), row(j + 2, 0), row(j, 0)
+        h, h_n, h_s = row(j + 1, 2), row(j + 2, 2), row(j, 2)
         v, v_n, v_s = row(j + 1, 1), row(j + 2, 1), row(j, 1)
-        u = row(j + 1, 5)
+        u = row(j + 1, 0)
         h_e, h_w = eastward(h), westward(h)
         flux_e = 0.5 * (u + eastward(u)) * (0.5 * (h + h_e))
         flux_w = 0.5 * (westward(u) + u) * (0.5 * (h_w + h))
@@ -343,30 +343,17 @@
         inverse, sine, cos_north, cos_south = scalars(j)
         h, u, v, h_e, h_w, h_n, h_s, flux_e, flux_w, flux_n, flux_s = fluxes(j, cos_north, cos_south)
         for c in range(3):
-            q, q_n, q_s = row(j + 1, 2 + c), row(j + 2, 2 + c), row(j, 2 + c)
+            q, q_n, q_s = row(j + 1, 3 + c), row(j + 2, 3 + c), row(j, 3 + c)
             q_e, q_w = eastward(q), westward(q)
             zonal = flux_e * (0.5 * (q + q_e)) - flux_w * (0.5 * (q_w + q))
             merid = flux_n * (0.5 * (q + q_n)) - flux_s * (0.5 * (q_s + q))
             flux = (zonal + RATIO * merid) * inverse
             laplace = (q_e + q_w) + (q_n + q_s) - 4.0 * q
-            at = pl.ds(pl.multiple_of((c * ROWS + j) * TILES, 8), TILES)
+            at = pl.ds(pl.multiple_of((j * 3 + c) * TILES, 8), TILES)
             mass[at, :] = h * q + TIME_STEP * (DIFFUSION * laplace - flux)
         return carry
 
     lax.fori_loop(0, ROWS, tracer, 0)
-
-    def narrow(t, carry):
-        at = pl.ds(pl.multiple_of(t * LANES, LANES), LANES)
-        for c in range(3):
-            mv[c, :, at] = mass[pl.ds(c * ROWS * TILES + t, ROWS, stride=TILES), :].astype(BF16)
-        return carry
-
-    lax.fori_loop(0, FULL, narrow, 0)
-    for c in range(3):
-        last = mass[pl.ds(c * ROWS * TILES + FULL, ROWS, stride=TILES), :]
-        mv[c, :, pl.ds(FULL * LANES, TAIL)] = last[:, :TAIL].astype(BF16)
-    stores = [pltpu.make_async_copy(mv, mass_out, out_sem.at[0])]
-    stores[0].start()
 
     for load in tables:
         load.wait()
@@ -429,37 +416,10 @@
 
         lax.fori_loop(0, N_LON, away, 0)
 
-    def update(source):
-        def whole(t, carry):
-            at = pl.ds(pl.multiple_of(t * LANES, LANES), LANES)
-            step = [source[pl.ds(f * TILES + t, ROWS, stride=3 * TILES), :] for f in range(3)]
-            hv[:, at] = hv[:, at] + TIME_STEP * step[0]
-            wv[0, :, at] = wv[0, :, at] + TIME_STEP * step[1]
-            wv[1, :, at] = wv[1, :, at] + TIME_STEP * step[2]
-            return carry
-
-        lax.fori_loop(0, FULL, whole, 0)
-        at = pl.ds(FULL * LANES, TAIL)
-        step = [source[pl.ds(f * TILES + FULL, ROWS, stride=3 * TILES), :][:, :TAIL] for f in range(3)]
-        hv[:, at] = hv[:, at] + TIME_STEP * step[0]
-        wv[0, :, at] = wv[0, :, at] + TIME_STEP * step[1]
-        wv[1, :, at] = wv[1, :, at] + TIME_STEP * step[2]
-
-    @pl.when(polar)
-    def _():
-        wait_for(returned, PAIRS - 1, back_recv)
-        update(returned)
-
     @pl.when(jnp.logical_not(polar))
     def _():
-        update(tend)
-
-    stores += [
-        pltpu.make_async_copy(wv, winds_out, out_sem.at[1]),
-        pltpu.make_async_copy(hv, thick_out, out_sem.at[2]),
-    ]
-    stores[1].start()
-    stores[2].start()
+        returned[...] = tend[...]
+
     halos[2].wait_send()
     halos[3].wait_send()
 
@@ -467,54 +427,79 @@
     def _():
         wait_for(tend, PAIRS - 1, go_send)
         wait_for(sent_back, N_LON - 1, back_send)
+        wait_for(returned, PAIRS - 1, back_recv)
 
     @pl.when(lends)
     def _():
         wait_for(sent_back, N_LON, back_send)
 
-    for store in stores:
-        store.wait()
+
+def finish(winds, thick, steps, mass, winds_out, thick_out, mass_out):
+    def one_row(j, carry):
+        start = j * 3 * TILES
+        for t in range(FULL + 1):
+            width = LANES if t < FULL else TAIL
+            at = pl.ds(t * LANES, width)
+            step = steps[pl.ds(start + TILES + t, 2, stride=TILES), :]
+            winds_out[j, :, at] = winds[j, :, at] + TIME_STEP * step[:, :width]
+            mass_out[j, :, at] = mass[pl.ds(start + t, 3, stride=TILES), :][:, :width].astype(BF16)
+        return carry
+
+    lax.fori_loop(0, ROWS, one_row, 0)
+    for t in range(FULL + 1):
+        width = LANES if t < FULL else TAIL
+        at = pl.ds(t * LANES, width)
+        thick_out[:, at] = thick[:, at] + TIME_STEP * steps[pl.ds(t, ROWS, stride=3 * TILES), :][:, :width]
 
 
 def local(winds, thickness, tracers, cutoff):
     fore, twiddle, mix, unmix, back = filter_tables()
     anywhere = pl.BlockSpec(memory_space=pl.ANY)
     scalar = pl.BlockSpec(memory_space=pltpu.SMEM)
+    whole = pl.BlockSpec(memory_space=pltpu.VMEM)
     side = pltpu.VMEM((48, LANES), F32)
     dma = pltpu.SemaphoreType.DMA
-    return pl.pallas_call(
+    rows = jax.ShapeDtypeStruct((PAIRS * BLOCK, LANES), F32)
+    winds = jnp.transpose(winds, (1, 0, 2))
+    tracers = jnp.transpose(tracers, (1, 0, 2))
+    steps, mass = pl.pallas_call(
         kernel,
-        out_shape=(
-            jax.ShapeDtypeStruct((2, ROWS, WIDE), F32),
-            jax.ShapeDtypeStruct((ROWS, WIDE), F32),
-            jax.ShapeDtypeStruct((3, ROWS, WIDE), BF16),
-        ),
+        out_shape=(rows, rows),
         in_specs=[scalar, scalar] + [anywhere] * 8,
-        out_specs=(anywhere,) * 3,
+        out_specs=(whole, whole),
         scratch_shapes=[
-            pltpu.VMEM((2, ROWS, WIDE), F32),
+            pltpu.VMEM((ROWS, 2, WIDE), F32),
             pltpu.VMEM((ROWS, WIDE), F32),
-            pltpu.VMEM((3, ROWS, WIDE), BF16),
-            pltpu.VMEM((3, ROWS, WIDE), BF16),
+            pltpu.VMEM((ROWS, 3, WIDE), BF16),
             pltpu.VMEM(((ROWS + 2) * SLOT, LANES), F32),
             side, side, side, side,
             pltpu.VMEM((PAIRS * BLOCK, LANES), F32),
             pltpu.VMEM((N_LON * BLOCK, LANES), F32),
             pltpu.VMEM((N_LON * BLOCK, LANES), F32),
-            pltpu.VMEM((PAIRS * BLOCK, LANES), F32),
-            pltpu.VMEM((PAIRS * BLOCK, LANES), F32),
             pltpu.VMEM(fore.shape, BF16),
             pltpu.VMEM(twiddle.shape, F32),
             pltpu.VMEM(mix.shape, BF16),
             pltpu.VMEM(unmix.shape, BF16),
             pltpu.VMEM(back.shape, BF16),
-            dma((3,)), dma((5,)), dma((3,)), dma((4,)), dma((4,)), dma, dma, dma, dma,
+            dma((3,)), dma((5,)), dma((4,)), dma((4,)), dma, dma, dma, dma,
         ],
         compiler_params=pltpu.CompilerParams(
-            collective_id=0, has_side_effects=True, vmem_limit_bytes=40 * 1024 * 1024
+            collective_id=0, has_side_effects=True, vmem_limit_bytes=VMEM_MIB * 1024 * 1024
         ),
         name="substep",
     )(cutoff, geometry(), winds, thickness, tracers, fore, twiddle, mix, unmix, back)
+    new_winds, new_thickness, new_mass = pl.pallas_call(
+        finish,
+        out_shape=(
+            jax.ShapeDtypeStruct((ROWS, 2, WIDE), F32),
+            jax.ShapeDtypeStruct((ROWS, WIDE), F32),
+            jax.ShapeDtypeStruct((ROWS, 3, WIDE), BF16),
+        ),
+        in_specs=[whole] * 4,
+        out_specs=(whole,) * 3,
+        name="finish",
+    )(winds, thickness, steps, mass)
+    return jnp.transpose(new_winds, (1, 0, 2)), new_thickness, jnp.transpose(new_mass, (1, 0, 2))
 
 
 def solution(mesh):

time: 44.4 us -> 37.9 us (0.85)
  local copies, waits for them, and re-layouts: 8.14 us -> 0 us
  Pallas kernels: 35.3 us -> 37.1 us
    unnamed x19 -> x0, local copies, waits for them, and re-layouts: 6.58 us -> none
    pallas_call x1 -> x2, Pallas kernels: 35.3 us -> 37.1 us  [the longest x1 34.6 us: local(): pl.pallas_call(kernel, out_shape=(rows, rows), in_specs=[scalar, scalar]...]
    pallas_call x2 -> x0, local copies, waits for them, and re-layouts: 1.56 us -> none  [local(): pl.pallas_call(kernel, out_shape=(jax.ShapeDtypeStruct((2, ROWS, WIDE), F...]
where the time goes in v1:
time: 37.9 us; the launch traced here: 37.7 us
  Pallas kernels  37.1 us (98%)
  between operations  0.64 us (2%)
    pallas_call x1, Pallas kernels, local(): pl.pallas_call(kernel, out_shape=(rows, rows), in_specs=[scalar, scalar]...  34.6 us
    pallas_call x1, Pallas kernels, local(): pl.pallas_call(finish, out_shape=(jax.ShapeDtypeStruct((ROWS, 2, WIDE), F...  2.49 us

profile of v1, /device:TPU:1, one launch (start us, length us, event | category | flops | bytes accessed | tf_op | source)
XLA Modules:
  0.0 37.7 jit_solution(3171481699021889136)
XLA Ops:
  0.6 34.6 %substep.1 = (f32[648,128]{1,0:T(8,128)}, f32[648,128]{1,0:T(8,128)}) custom-call(s32[288]{0:T(512)} %cut.1, f32[1152]{0:T(1024)} %constant.12.clone.geo, f32[9,2,2880]{2,1,0:T(2,128)} %bitcast.4, f32[9,2880]{1,0:T(8,128)} %thick.1, bf16[9,3,2880]{2,1,0:T(4,128)(2,1)} %bitcast.6, bf16[736,192]{1,0:T(8,128)(2,1)} %constant.13.clone.fore_in, ...), custom_call_target="tpu_custom_call" | custom-call | tf_op jit(solution)/shard_map/substep/pallas_call | solution.py:465
  35.2 2.5 %finish.1 = (f32[9,2,2880]{2,1,0:T(2,128)}, f32[9,2880]{1,0:T(8,128)}, bf16[9,3,2880]{2,1,0:T(4,128)(2,1)}) custom-call(f32[9,2,2880]{2,1,0:T(2,128)} %bitcast.5, f32[9,2880]{1,0:T(8,128)} %thick.1, f32[648,128]{1,0:T(8,128)} %get-tuple-element.8.steps, f32[648,128]{1,0:T(8,128)} %get-tuple-element.9.mass), custom_call_target="tpu_custom_call" | custom-call | tf_op jit(solution)/shard_map/finish/pallas_call | solution.py:491

commit v2 on v1

--- a/solution.py
+++ b/solution.py
@@ -36,8 +36,8 @@
 SLOT = FIELDS * TILES
 EDGE = 5 * TILES
 PAIRS = 3 * ROWS
-BLOCK = TILES
-OWN = N_LON
+BLOCK = FULL + 1
+OWN = 14
 AWAY = PAIRS - OWN
 
 BASE = NLON // PER
@@ -128,10 +128,10 @@
 
 
 def kernel(
-    cut, geo, winds_in, thick_in, mass_in, fore_in, twiddle_in, mix_in, unmix_in, back_in,
+    cut_in, geo_in, winds_in, thick_in, mass_in, fore_in, twiddle_in, mix_in, unmix_in, back_in,
     returned, mass,
     wv, hv, qv, cells, to_east, to_west, from_west, from_east, tend, gathered, sent_back,
-    fore, twiddle, mix, unmix, back,
+    fore, twiddle, mix, unmix, back, cut, geo,
     in_sem, table_sem, halo_send, halo_recv, go_send, go_recv, back_send, back_recv,
 ):
     lat = lax.axis_index("lat")
@@ -141,15 +141,44 @@
     polar = jnp.logical_or(polar_south, polar_north)
     other = (lat + N_LAT // 2) % N_LAT
     other_polar = jnp.logical_or(other * ROWS < POLAR, (other + 1) * ROWS > NLAT - POLAR)
+    works = jnp.logical_and(polar, lon < OWN)
     lends = jnp.logical_and(other_polar, lon < AWAY)
+
+    east = (lat, (lon + 1) % N_LON)
+    west = (lat, (lon + N_LON - 1) % N_LON)
+    below = (lat + N_LAT - 1) // N_LAT
+    above = 1 - lat // (N_LAT - 1)
+    south = (lat - below, (lon + (1 - below) * (N_LON // 2)) % N_LON)
+    north = (lat + above, (lon + (1 - above) * (N_LON // 2)) % N_LON)
+
+    barrier = pltpu.get_barrier_semaphore()
+
+    def greet(device):
+        pl.semaphore_signal(barrier, inc=1, device_id=device, device_id_type=MESH)
+
+    for device in (east, west, south, north):
+        greet(device)
+
+    @pl.when(polar)
+    def _():
+        lax.fori_loop(1, N_LON, lambda i, c: (greet((lat, (lon + i) % N_LON)), c)[1], 0)
+        lax.fori_loop(0, AWAY, lambda i, c: (greet((other, i)), c)[1], 0)
+
+    @pl.when(lends)
+    def _():
+        lax.fori_loop(0, N_LON, lambda i, c: (greet((other, i)), c)[1], 0)
 
     loads = [
         pltpu.make_async_copy(winds_in, wv, in_sem.at[0]),
         pltpu.make_async_copy(thick_in, hv, in_sem.at[1]),
         pltpu.make_async_copy(mass_in, qv, in_sem.at[2]),
+        pltpu.make_async_copy(geo_in, geo, in_sem.at[3]),
+        pltpu.make_async_copy(cut_in, cut, in_sem.at[4]),
     ]
     for load in loads:
         load.start()
+    for load in loads:
+        load.wait()
     tables = [
         pltpu.make_async_copy(source, target, table_sem.at[i])
         for i, (source, target) in enumerate(
@@ -158,33 +187,6 @@
     ]
     for load in tables:
         load.start()
-
-    east = (lat, (lon + 1) % N_LON)
-    west = (lat, (lon + N_LON - 1) % N_LON)
-    below = (lat + N_LAT - 1) // N_LAT
-    above = 1 - lat // (N_LAT - 1)
-    south = (lat - below, (lon + (1 - below) * (N_LON // 2)) % N_LON)
-    north = (lat + above, (lon + (1 - above) * (N_LON // 2)) % N_LON)
-
-    barrier = pltpu.get_barrier_semaphore()
-
-    def greet(device):
-        pl.semaphore_signal(barrier, inc=1, device_id=device, device_id_type=MESH)
-
-    for device in (east, west, south, north):
-        greet(device)
-
-    @pl.when(polar)
-    def _():
-        lax.fori_loop(1, N_LON, lambda i, c: (greet((lat, (lon + i) % N_LON)), c)[1], 0)
-        lax.fori_loop(0, AWAY, lambda i, c: (greet((other, i)), c)[1], 0)
-
-    @pl.when(lends)
-    def _():
-        lax.fori_loop(0, N_LON, lambda i, c: (greet((other, i)), c)[1], 0)
-
-    for load in loads:
-        load.wait()
 
     def padded(value):
         return jnp.concatenate([value, jnp.zeros((value.shape[0], LANES - TAIL), F32)], axis=1)
@@ -198,6 +200,7 @@
                 wind, ratio = padded(wind), padded(ratio)
             cells[pl.ds(start + t, 2, stride=TILES), :] = wind
             cells[pl.ds(start + 3 * TILES + t, 3, stride=TILES), :] = ratio
+        cells[pl.ds(start + FULL + 1, FIELDS, stride=TILES), :] = jnp.zeros((FIELDS, LANES), F32)
         return carry
 
     lax.fori_loop(0, ROWS, place_row, 0)
@@ -211,6 +214,83 @@
         last = cells[pl.ds(SLOT + f * TILES + FULL, ROWS, stride=SLOT), :]
         to_west[pl.ds(i * ROWS, ROWS), :] = pltpu.roll(first, TAIL, 1)
         to_east[pl.ds(i * ROWS, ROWS), :] = pltpu.roll(last, LANES - TAIL, 1)
+
+    gathered[pl.ds(FULL + 1, N_LON, stride=TILES), :] = jnp.zeros((N_LON, LANES), F32)
+
+    def row(slot, field):
+        return cells[pl.ds(pl.multiple_of(slot * SLOT + field * TILES, 8), TILES), :]
+
+    def scalars(j):
+        at = (lat * ROWS + j) * 4
+        return geo[at], geo[at + 1], geo[at + 2], geo[at + 3]
+
+    flat = lax.broadcasted_iota(jnp.int32, (TILES, LANES), 0) * LANES + lax.broadcasted_iota(
+        jnp.int32, (TILES, LANES), 1
+    )
+    valid = flat < WIDE
+
+    def fluxes(j, cos_north, cos_south):
+        h, h_n, h_s = row(j + 1, 2), row(j + 2, 2), row(j, 2)
+        v, v_n, v_s = row(j + 1, 1), row(j + 2, 1), row(j, 1)
+        u = row(j + 1, 0)
+        h_e, h_w = eastward(h), westward(h)
+        flux_e = 0.5 * (u + eastward(u)) * (0.5 * (h + h_e))
+        flux_w = 0.5 * (westward(u) + u) * (0.5 * (h_w + h))
+        flux_n = 0.5 * (v + v_n) * (0.5 * (h + h_n)) * cos_north
+        flux_s = 0.5 * (v_s + v) * (0.5 * (h_s + h)) * cos_south
+        return h, u, v, h_e, h_w, h_n, h_s, flux_e, flux_w, flux_n, flux_s
+
+    lane = lax.broadcasted_iota(jnp.int32, (ROWS, LANES), 1)
+
+    def keep_row(j, f, target, value):
+        at = pl.ds(pl.multiple_of((j * 3 + f) * TILES, 8), TILES)
+        target[at, :] = jnp.where(valid, value, 0.0)
+
+    def along(j):
+        inverse, sine = scalars(j)[:2]
+        h, v = row(j + 1, 2), row(j + 1, 1)
+        return sine * v - (eastward(h) - westward(h)) * (0.5 * inverse)
+
+    def tendency(j, target, both):
+        inverse, sine, cos_north, cos_south = scalars(j)
+        h, u, v, h_e, h_w, h_n, h_s, flux_e, flux_w, flux_n, flux_s = fluxes(j, cos_north, cos_south)
+        keep_row(j, 0, target, -((flux_e - flux_w) + RATIO * (flux_n - flux_s)) * inverse)
+        if both:
+            keep_row(j, 1, target, sine * v - (h_e - h_w) * (0.5 * inverse))
+        keep_row(j, 2, target, -sine * u - RATIO * (h_n - h_s) * 0.5)
+
+    def corner():
+        def column(field, tile, lanes):
+            value = cells[pl.ds(SLOT + field * TILES + tile, ROWS, stride=SLOT), :]
+            return pltpu.roll(value, lanes, 1)
+
+        last = TAIL - LEVELS
+        value = jnp.where(lane < TAIL + LEVELS, column(2, 0, TAIL), column(2, FULL, TAIL + LEVELS - last))
+        value = jnp.where(lane < TAIL + 2 * LEVELS, value, column(0, 0, TAIL + 2 * LEVELS))
+        return jnp.where(lane < TAIL + 3 * LEVELS, value, column(0, FULL, TAIL + 3 * LEVELS - last))
+
+    @pl.when(polar)
+    def _():
+        lax.fori_loop(1, ROWS - 1, lambda j, c: (tendency(j, tend, True), c)[1], 0)
+        for j in (0, ROWS - 1):
+            keep_row(j, 1, tend, along(j))
+        value = corner()
+        at = pl.ds(TILES + FULL, ROWS, stride=3 * TILES)
+        tend[at, :] = jnp.where(lane < TAIL, tend[at, :], value)
+        at = pl.ds(3 * TILES + FULL, ROWS - 2, stride=3 * TILES)
+        inner = slice(1, ROWS - 1)
+        tend[at, :] = jnp.where(lane[inner] < TAIL, tend[at, :], value[inner])
+
+    def block(ref, index):
+        return ref.at[pl.ds(pl.multiple_of(index * TILES, 8), BLOCK), :]
+
+    def place(sector):
+        return (sector % 2) * (N_LON // 2) + sector // 2
+
+    def go(pair, device):
+        return pltpu.make_async_remote_copy(
+            block(tend, pair), block(gathered, place(lon)), go_send, go_recv, device_id=device, device_id_type=MESH
+        )
 
     @pl.when(polar)
     def _():
@@ -247,119 +327,107 @@
     ]
     for halo in halos:
         halo.start()
-    pltpu.make_async_copy(edge(0), edge(0), halo_recv.at[0]).wait()
-    pltpu.make_async_copy(edge(ROWS + 1), edge(ROWS + 1), halo_recv.at[1]).wait()
-    pltpu.make_async_copy(from_west, from_west, halo_recv.at[2]).wait()
-    pltpu.make_async_copy(from_east, from_east, halo_recv.at[3]).wait()
-    halos[0].wait_send()
-    halos[1].wait_send()
-
-    lane = lax.broadcasted_iota(jnp.int32, (ROWS, LANES), 1)
-    for i, f in enumerate(sides):
-        at = pl.ds(SLOT + f * TILES + FULL, ROWS, stride=SLOT)
-        here = from_east[pl.ds(i * ROWS, ROWS), :]
-        cells[at, :] = jnp.where((lane >= TAIL) & (lane < TAIL + LEVELS), here, cells[at, :])
-        at = pl.ds(SLOT + f * TILES + FULL + 1, ROWS, stride=SLOT)
-        here = from_west[pl.ds(i * ROWS, ROWS), :]
-        cells[at, :] = jnp.where(lane >= LANES - LEVELS, here, 0.0)
-
-    @pl.when(lat == 0)
-    def _():
-        at = pl.ds(TILES, TILES)
-        cells[at, :] = -cells[at, :]
-
-    @pl.when(lat == N_LAT - 1)
-    def _():
-        at = pl.ds((ROWS + 1) * SLOT + TILES, TILES)
-        cells[at, :] = -cells[at, :]
-
-    def row(slot, field):
-        return cells[pl.ds(pl.multiple_of(slot * SLOT + field * TILES, 8), TILES), :]
-
-    def scalars(j):
-        at = (lat * ROWS + j) * 4
-        return geo[at], geo[at + 1], geo[at + 2], geo[at + 3]
-
-    flat = lax.broadcasted_iota(jnp.int32, (TILES, LANES), 0) * LANES + lax.broadcasted_iota(
-        jnp.int32, (TILES, LANES), 1
-    )
-    valid = flat < WIDE
-
-    def fluxes(j, cos_north, cos_south):
-        h, h_n, h_s = row(j + 1, 2), row(j + 2, 2), row(j, 2)
-        v, v_n, v_s = row(j + 1, 1), row(j + 2, 1), row(j, 1)
-        u = row(j + 1, 0)
-        h_e, h_w = eastward(h), westward(h)
-        flux_e = 0.5 * (u + eastward(u)) * (0.5 * (h + h_e))
-        flux_w = 0.5 * (westward(u) + u) * (0.5 * (h_w + h))
-        flux_n = 0.5 * (v + v_n) * (0.5 * (h + h_n)) * cos_north
-        flux_s = 0.5 * (v_s + v) * (0.5 * (h_s + h)) * cos_south
-        return h, u, v, h_e, h_w, h_n, h_s, flux_e, flux_w, flux_n, flux_s
-
-    def tendency(j, carry):
-        inverse, sine, cos_north, cos_south = scalars(j)
-        h, u, v, h_e, h_w, h_n, h_s, flux_e, flux_w, flux_n, flux_s = fluxes(j, cos_north, cos_south)
-        values = (
-            -((flux_e - flux_w) + RATIO * (flux_n - flux_s)) * inverse,
-            sine * v - (h_e - h_w) * (0.5 * inverse),
-            -sine * u - RATIO * (h_n - h_s) * 0.5,
-        )
-        for f, value in enumerate(values):
-            at = pl.ds(pl.multiple_of((j * 3 + f) * BLOCK, 8), BLOCK)
-            tend[at, :] = jnp.where(valid, value, 0.0)
-        return carry
-
-    lax.fori_loop(0, ROWS, tendency, 0)
-
-    def block(ref, index):
-        return ref.at[pl.ds(pl.multiple_of(index * BLOCK, 8), BLOCK), :]
-
-    def place(sector):
-        return (sector % 2) * (N_LON // 2) + sector // 2
-
-    def go(pair, device):
-        return pltpu.make_async_remote_copy(
-            block(tend, pair), block(gathered, place(lon)), go_send, go_recv, device_id=device, device_id_type=MESH
-        )
+
+    def rows_arrive():
+        pltpu.make_async_copy(edge(0), edge(0), halo_recv.at[0]).wait()
+        pltpu.make_async_copy(edge(ROWS + 1), edge(ROWS + 1), halo_recv.at[1]).wait()
+
+        @pl.when(lat == 0)
+        def _():
+            at = pl.ds(TILES, TILES)
+            cells[at, :] = -cells[at, :]
+
+        @pl.when(lat == N_LAT - 1)
+        def _():
+            at = pl.ds((ROWS + 1) * SLOT + TILES, TILES)
+            cells[at, :] = -cells[at, :]
+
+    def send(pair):
+        if pair < OWN:
+
+            @pl.when(lon != pair)
+            def _():
+                go(pair, (lat, pair)).start()
+        else:
+            go(pair, (other, pair - OWN)).start()
+
+    late = (0, 2, PAIRS - 3, PAIRS - 1)
+
+    def is_early(pair):
+        ready = pair != late[0]
+        for other_pair in late[1:]:
+            ready = jnp.logical_and(ready, pair != other_pair)
+        return ready
 
     @pl.when(polar)
     def _():
-        def own(i, carry):
-            target = (lon + i) % N_LON
-            go(target, (lat, target)).start()
+        def early(i, carry):
+            near = (lon + i) % N_LON
+
+            @pl.when(jnp.logical_and(jnp.logical_and(near < OWN, near != lon), is_early(near)))
+            def _():
+                go(near, (lat, near)).start()
+
+            far = (lon + i) % N_LON
+
+            @pl.when(jnp.logical_and(far < AWAY, is_early(far + OWN)))
+            def _():
+                go(far + OWN, (other, far)).start()
+
             return carry
 
-        def away(i, carry):
-            target = (lon + i) % AWAY
-            go(OWN + target, (other, target)).start()
-            return carry
-
-        lax.fori_loop(0, AWAY, away, 0)
-        lax.fori_loop(1, N_LON, own, 0)
-        at = pl.ds(pl.multiple_of(place(lon) * BLOCK, 8), BLOCK)
-        gathered[at, :] = tend[pl.ds(pl.multiple_of(lon * BLOCK, 8), BLOCK), :]
-
-    def tracer(j, carry):
-        inverse, sine, cos_north, cos_south = scalars(j)
-        h, u, v, h_e, h_w, h_n, h_s, flux_e, flux_w, flux_n, flux_s = fluxes(j, cos_north, cos_south)
-        for c in range(3):
-            q, q_n, q_s = row(j + 1, 3 + c), row(j + 2, 3 + c), row(j, 3 + c)
-            q_e, q_w = eastward(q), westward(q)
-            zonal = flux_e * (0.5 * (q + q_e)) - flux_w * (0.5 * (q_w + q))
-            merid = flux_n * (0.5 * (q + q_n)) - flux_s * (0.5 * (q_s + q))
-            flux = (zonal + RATIO * merid) * inverse
-            laplace = (q_e + q_w) + (q_n + q_s) - 4.0 * q
-            at = pl.ds(pl.multiple_of((j * 3 + c) * TILES, 8), TILES)
-            mass[at, :] = h * q + TIME_STEP * (DIFFUSION * laplace - flux)
-        return carry
-
-    lax.fori_loop(0, ROWS, tracer, 0)
-
-    for load in tables:
-        load.wait()
-
-    def circle(pair_row):
-        cutoff = cut[pair_row]
+        lax.fori_loop(0, N_LON, early, 0)
+        rows_arrive()
+        for j in (0, ROWS - 1):
+            tendency(j, tend, False)
+        value = corner()
+        for j in (0, ROWS - 1):
+            at = pl.ds(3 * j * TILES + FULL, 1)
+            tend[at, :] = jnp.where(lane[:1] < TAIL, tend[at, :], value[j : j + 1])
+        for pair in late:
+            send(pair)
+
+    @pl.when(works)
+    def _():
+        at = pl.ds(pl.multiple_of(place(lon) * TILES, 8), BLOCK)
+        gathered[at, :] = tend[pl.ds(pl.multiple_of(lon * TILES, 8), BLOCK), :]
+
+    def complete(pair, lat_row):
+        inverse = geo[lat_row * 4]
+        first_at, last_at = pl.ds(0, N_LON, stride=TILES), pl.ds(FULL, N_LON, stride=TILES)
+        first, last = gathered[first_at, :], gathered[last_at, :]
+        spot = lax.broadcasted_iota(jnp.int32, (N_LON, LANES), 1)
+        half = N_LON // 2
+        after = jnp.concatenate([last[half:], pltpu.roll(last[:half], half - 1, 0)], axis=0)
+        before = jnp.concatenate([pltpu.roll(last[half:], 1, 0), last[:half]], axis=0)
+
+        def pick(value, part, to):
+            return pltpu.roll(value, (LANES + to - TAIL - part * LEVELS) % LANES, 1)
+
+        end = TAIL - LEVELS
+        h_first, h_end, u_first, u_end = 0, 1, 2, 3
+        field = pair % 3
+
+        def put(east, west):
+            gathered[last_at, :] = jnp.where(spot < end, last, jnp.where(spot < TAIL, last + east, 0.0))
+            gathered[first_at, :] = jnp.where(spot < LEVELS, first + west, first)
+
+        @pl.when(field == 0)
+        def _():
+            h, u = pick(last, h_end, end), pick(last, u_end, end)
+            east = (u + pick(after, u_first, end)) * (h + pick(after, h_first, end)) - u * h
+            h, u = pick(last, h_first, 0), pick(last, u_first, 0)
+            west = (u + pick(before, u_end, 0)) * (h + pick(before, h_end, 0)) - u * h
+            put(-0.25 * inverse * east, 0.25 * inverse * west)
+
+        @pl.when(field == 1)
+        def _():
+            put(-0.5 * inverse * pick(after, h_first, end), 0.5 * inverse * pick(before, h_end, 0))
+
+    def circle(pair, first_row):
+        lat_row = first_row + pair // 3
+        complete(pair, lat_row)
+        cutoff = cut[lat_row]
         data = jnp.concatenate([gathered[pl.ds(0, SIDE), :], gathered[pl.ds(SIDE, SIDE), :]], axis=1)
         lines = table_left(fore, 2 * FREQ, data)
         real, imag = lines[:FREQ], lines[FREQ:]
@@ -390,10 +458,65 @@
     def wait_for(ref, blocks, sem):
         pltpu.make_async_copy(total(ref, blocks), total(ref, blocks), sem).wait()
 
-    @pl.when(polar)
+    @pl.when(lends)
+    def _():
+        for load in tables:
+            load.wait()
+        wait_for(gathered, N_LON, go_recv)
+        circle(OWN + lon, other * ROWS)
+
+        def away(i, carry):
+            target = (lon + i) % N_LON
+            home(OWN + lon, target, (other, target)).start()
+            return carry
+
+        lax.fori_loop(0, N_LON, away, 0)
+
+    @pl.when(jnp.logical_not(polar))
+    def _():
+        rows_arrive()
+
+    pltpu.make_async_copy(from_west, from_west, halo_recv.at[2]).wait()
+    pltpu.make_async_copy(from_east, from_east, halo_recv.at[3]).wait()
+    halos[0].wait_send()
+    halos[1].wait_send()
+    for i, f in enumerate(sides):
+        at = pl.ds(SLOT + f * TILES + FULL, ROWS, stride=SLOT)
+        here = from_east[pl.ds(i * ROWS, ROWS), :]
+        cells[at, :] = jnp.where((lane >= TAIL) & (lane < TAIL + LEVELS), here, cells[at, :])
+        at = pl.ds(SLOT + f * TILES + FULL + 1, ROWS, stride=SLOT)
+        here = from_west[pl.ds(i * ROWS, ROWS), :]
+        cells[at, :] = jnp.where(lane >= LANES - LEVELS, here, 0.0)
+
+    @pl.when(jnp.logical_not(polar))
+    def _():
+        lax.fori_loop(0, ROWS, lambda j, c: (tendency(j, returned, True), c)[1], 0)
+
+    def tracer(j, carry):
+        inverse, sine, cos_north, cos_south = scalars(j)
+        h, u, v, h_e, h_w, h_n, h_s, flux_e, flux_w, flux_n, flux_s = fluxes(j, cos_north, cos_south)
+        for c in range(3):
+            q, q_n, q_s = row(j + 1, 3 + c), row(j + 2, 3 + c), row(j, 3 + c)
+            q_e, q_w = eastward(q), westward(q)
+            zonal = flux_e * (0.5 * (q + q_e)) - flux_w * (0.5 * (q_w + q))
+            merid = flux_n * (0.5 * (q + q_n)) - flux_s * (0.5 * (q_s + q))
+            flux = (zonal + RATIO * merid) * inverse
+            laplace = (q_e + q_w) + (q_n + q_s) - 4.0 * q
+            at = pl.ds(pl.multiple_of((j * 3 + c) * TILES, 8), TILES)
+            mass[at, :] = h * q + TIME_STEP * (DIFFUSION * laplace - flux)
+        return carry
+
+    lax.fori_loop(0, ROWS, tracer, 0)
+
+    @pl.when(jnp.logical_not(lends))
+    def _():
+        for load in tables:
+            load.wait()
+
+    @pl.when(works)
     def _():
         wait_for(gathered, N_LON - 1, go_recv)
-        circle(lat * ROWS + lon // 3)
+        circle(lon, lat * ROWS)
 
         def own(i, carry):
             target = (lon + i) % N_LON
@@ -401,33 +524,22 @@
             return carry
 
         lax.fori_loop(1, N_LON, own, 0)
-        at = pl.ds(pl.multiple_of(place(lon) * BLOCK, 8), BLOCK)
-        returned[pl.ds(pl.multiple_of(lon * BLOCK, 8), BLOCK), :] = sent_back[at, :]
-
-    @pl.when(lends)
-    def _():
-        wait_for(gathered, N_LON, go_recv)
-        circle(other * ROWS + (OWN + lon) // 3)
-
-        def away(i, carry):
-            target = (lon + i) % N_LON
-            home(OWN + lon, target, (other, target)).start()
-            return carry
-
-        lax.fori_loop(0, N_LON, away, 0)
-
-    @pl.when(jnp.logical_not(polar))
-    def _():
-        returned[...] = tend[...]
+        at = pl.ds(pl.multiple_of(place(lon) * TILES, 8), BLOCK)
+        returned[pl.ds(pl.multiple_of(lon * TILES, 8), BLOCK), :] = sent_back[at, :]
 
     halos[2].wait_send()
     halos[3].wait_send()
 
-    @pl.when(polar)
+    @pl.when(works)
     def _():
         wait_for(tend, PAIRS - 1, go_send)
         wait_for(sent_back, N_LON - 1, back_send)
         wait_for(returned, PAIRS - 1, back_recv)
+
+    @pl.when(jnp.logical_and(polar, lon >= OWN))
+    def _():
+        wait_for(tend, PAIRS, go_send)
+        wait_for(returned, PAIRS, back_recv)
 
     @pl.when(lends)
     def _():
@@ -455,17 +567,16 @@
 def local(winds, thickness, tracers, cutoff):
     fore, twiddle, mix, unmix, back = filter_tables()
     anywhere = pl.BlockSpec(memory_space=pl.ANY)
-    scalar = pl.BlockSpec(memory_space=pltpu.SMEM)
     whole = pl.BlockSpec(memory_space=pltpu.VMEM)
     side = pltpu.VMEM((48, LANES), F32)
     dma = pltpu.SemaphoreType.DMA
-    rows = jax.ShapeDtypeStruct((PAIRS * BLOCK, LANES), F32)
+    rows = jax.ShapeDtypeStruct((PAIRS * TILES, LANES), F32)
     winds = jnp.transpose(winds, (1, 0, 2))
     tracers = jnp.transpose(tracers, (1, 0, 2))
     steps, mass = pl.pallas_call(
         kernel,
         out_shape=(rows, rows),
-        in_specs=[scalar, scalar] + [anywhere] * 8,
+        in_specs=[anywhere] * 10,
         out_specs=(whole, whole),
         scratch_shapes=[
             pltpu.VMEM((ROWS, 2, WIDE), F32),
@@ -473,15 +584,17 @@
             pltpu.VMEM((ROWS, 3, WIDE), BF16),
             pltpu.VMEM(((ROWS + 2) * SLOT, LANES), F32),
             side, side, side, side,
-            pltpu.VMEM((PAIRS * BLOCK, LANES), F32),
-            pltpu.VMEM((N_LON * BLOCK, LANES), F32),
-            pltpu.VMEM((N_LON * BLOCK, LANES), F32),
+            pltpu.VMEM((PAIRS * TILES, LANES), F32),
+            pltpu.VMEM((N_LON * TILES, LANES), F32),
+            pltpu.VMEM((N_LON * TILES, LANES), F32),
             pltpu.VMEM(fore.shape, BF16),
             pltpu.VMEM(twiddle.shape, F32),
             pltpu.VMEM(mix.shape, BF16),
             pltpu.VMEM(unmix.shape, BF16),
             pltpu.VMEM(back.shape, BF16),
-            dma((3,)), dma((5,)), dma((4,)), dma((4,)), dma, dma, dma, dma,
+            pltpu.SMEM((NLAT,), jnp.int32),
+            pltpu.SMEM((4 * NLAT,), F32),
+            dma((5,)), dma((5,)), dma((4,)), dma((4,)), dma, dma, dma, dma,
         ],
         compiler_params=pltpu.CompilerParams(
             collective_id=0, has_side_effects=True, vmem_limit_bytes=VMEM_MIB * 1024 * 1024

time: 37.9 us -> 35 us (0.923)
  the two profiles are of different devices: /device:TPU:1 before, /device:TPU:66 now
where the time goes in v2:
time: 35 us; the launch traced here: 34.8 us
  Pallas kernels  34.2 us (98%)
  between operations  0.64 us (2%)
    pallas_call x1, Pallas kernels, local(): pl.pallas_call(kernel, out_shape=(rows, rows), in_specs=[anywhere] * 10,...  31.7 us
    pallas_call x1, Pallas kernels, local(): pl.pallas_call(finish, out_shape=(jax.ShapeDtypeStruct((ROWS, 2, WIDE), F...  2.49 us

profile of v2, /device:TPU:66, one launch (start us, length us, event | category | flops | bytes accessed | tf_op | source)
XLA Modules:
  0.0 34.8 jit_solution(4469122411550680666)
XLA Ops:
  0.6 31.7 %substep.1 = (f32[648,128]{1,0:T(8,128)}, f32[648,128]{1,0:T(8,128)}) custom-call(s32[288]{0:T(512)} %cut_in.1, f32[1152]{0:T(1024)} %constant.12.clone.geo_in, f32[9,2,2880]{2,1,0:T(2,128)} %bitcast.4, f32[9,2880]{1,0:T(8,128)} %thick.1, bf16[9,3,2880]{2,1,0:T(4,128)(2,1)} %bitcast.6, bf16[736,192]{1,0:T(8,128)(2,1)} %constant.13.clone.fore_in, ...), custom_call_target="tpu_custom_call" | custom-call | tf_op jit(solution)/shard_map/substep/pallas_call | solution.py:576
  32.3 2.5 %finish.1 = (f32[9,2,2880]{2,1,0:T(2,128)}, f32[9,2880]{1,0:T(8,128)}, bf16[9,3,2880]{2,1,0:T(4,128)(2,1)}) custom-call(f32[9,2,2880]{2,1,0:T(2,128)} %bitcast.5, f32[9,2880]{1,0:T(8,128)} %thick.1, f32[648,128]{1,0:T(8,128)} %get-tuple-element.8.steps, f32[648,128]{1,0:T(8,128)} %get-tuple-element.9.mass), custom_call_target="tpu_custom_call" | custom-call | tf_op jit(solution)/shard_map/finish/pallas_call | solution.py:604

commit v3 on v2

--- a/solution.py
+++ b/solution.py
@@ -37,7 +37,8 @@
 EDGE = 5 * TILES
 PAIRS = 3 * ROWS
 BLOCK = FULL + 1
-OWN = 14
+OWN = N_LON
+FAR = 12
 AWAY = PAIRS - OWN
 
 BASE = NLON // PER
@@ -141,7 +142,6 @@
     polar = jnp.logical_or(polar_south, polar_north)
     other = (lat + N_LAT // 2) % N_LAT
     other_polar = jnp.logical_or(other * ROWS < POLAR, (other + 1) * ROWS > NLAT - POLAR)
-    works = jnp.logical_and(polar, lon < OWN)
     lends = jnp.logical_and(other_polar, lon < AWAY)
 
     east = (lat, (lon + 1) % N_LON)
@@ -281,6 +281,15 @@
         inner = slice(1, ROWS - 1)
         tend[at, :] = jnp.where(lane[inner] < TAIL, tend[at, :], value[inner])
 
+    def partner(i):
+        ring = N_LON // 2
+        k = ring - 1 - i // 2
+        offset = (k + 1) // 2 * (2 * (k % 2) - 1)
+        return (lon // ring + i % 2) % 2 * ring + (lon % ring + offset + ring) % ring
+
+    def pair_of(i):
+        return (2 * i + PAIRS - 4) % PAIRS
+
     def block(ref, index):
         return ref.at[pl.ds(pl.multiple_of(index * TILES, 8), BLOCK), :]
 
@@ -342,15 +351,6 @@
             at = pl.ds((ROWS + 1) * SLOT + TILES, TILES)
             cells[at, :] = -cells[at, :]
 
-    def send(pair):
-        if pair < OWN:
-
-            @pl.when(lon != pair)
-            def _():
-                go(pair, (lat, pair)).start()
-        else:
-            go(pair, (other, pair - OWN)).start()
-
     late = (0, 2, PAIRS - 3, PAIRS - 1)
 
     def is_early(pair):
@@ -362,21 +362,19 @@
     @pl.when(polar)
     def _():
         def early(i, carry):
-            near = (lon + i) % N_LON
-
-            @pl.when(jnp.logical_and(jnp.logical_and(near < OWN, near != lon), is_early(near)))
+            near = partner(i)
+
+            @pl.when(jnp.logical_and(near != lon, is_early(pair_of(near))))
             def _():
-                go(near, (lat, near)).start()
-
-            far = (lon + i) % N_LON
-
-            @pl.when(jnp.logical_and(far < AWAY, is_early(far + OWN)))
+                go(pair_of(near), (lat, near)).start()
+
+            @pl.when(near < AWAY)
             def _():
-                go(far + OWN, (other, far)).start()
+                go(pair_of(OWN + near), (other, near)).start()
 
             return carry
 
-        lax.fori_loop(0, N_LON, early, 0)
+        lax.fori_loop(0, FAR, early, 0)
         rows_arrive()
         for j in (0, ROWS - 1):
             tendency(j, tend, False)
@@ -384,13 +382,18 @@
         for j in (0, ROWS - 1):
             at = pl.ds(3 * j * TILES + FULL, 1)
             tend[at, :] = jnp.where(lane[:1] < TAIL, tend[at, :], value[j : j + 1])
-        for pair in late:
-            send(pair)
-
-    @pl.when(works)
+        for target in (2, 3, N_LON - 2, N_LON - 1):
+
+            @pl.when(lon != target)
+            def _():
+                go(pair_of(target), (lat, target)).start()
+
+        lax.fori_loop(FAR, N_LON, early, 0)
+
+    @pl.when(polar)
     def _():
         at = pl.ds(pl.multiple_of(place(lon) * TILES, 8), BLOCK)
-        gathered[at, :] = tend[pl.ds(pl.multiple_of(lon * TILES, 8), BLOCK), :]
+        gathered[at, :] = tend[pl.ds(pl.multiple_of(pair_of(lon) * TILES, 8), BLOCK), :]
 
     def complete(pair, lat_row):
         inverse = geo[lat_row * 4]
@@ -463,11 +466,11 @@
         for load in tables:
             load.wait()
         wait_for(gathered, N_LON, go_recv)
-        circle(OWN + lon, other * ROWS)
+        circle(pair_of(OWN + lon), other * ROWS)
 
         def away(i, carry):
-            target = (lon + i) % N_LON
-            home(OWN + lon, target, (other, target)).start()
+            target = partner(i)
+            home(pair_of(OWN + lon), target, (other, target)).start()
             return carry
 
         lax.fori_loop(0, N_LON, away, 0)
@@ -513,33 +516,32 @@
         for load in tables:
             load.wait()
 
-    @pl.when(works)
+    @pl.when(polar)
     def _():
         wait_for(gathered, N_LON - 1, go_recv)
-        circle(lon, lat * ROWS)
+        circle(pair_of(lon), lat * ROWS)
 
         def own(i, carry):
-            target = (lon + i) % N_LON
-            home(lon, target, (lat, target)).start()
+            target = partner(i)
+
+            @pl.when(target != lon)
+            def _():
+                home(pair_of(lon), target, (lat, target)).start()
+
             return carry
 
-        lax.fori_loop(1, N_LON, own, 0)
+        lax.fori_loop(0, N_LON, own, 0)
         at = pl.ds(pl.multiple_of(place(lon) * TILES, 8), BLOCK)
-        returned[pl.ds(pl.multiple_of(lon * TILES, 8), BLOCK), :] = sent_back[at, :]
+        returned[pl.ds(pl.multiple_of(pair_of(lon) * TILES, 8), BLOCK), :] = sent_back[at, :]
 
     halos[2].wait_send()
     halos[3].wait_send()
 
-    @pl.when(works)
+    @pl.when(polar)
     def _():
         wait_for(tend, PAIRS - 1, go_send)
         wait_for(sent_back, N_LON - 1, back_send)
         wait_for(returned, PAIRS - 1, back_recv)
-
-    @pl.when(jnp.logical_and(polar, lon >= OWN))
-    def _():
-        wait_for(tend, PAIRS, go_send)
-        wait_for(returned, PAIRS, back_recv)
 
     @pl.when(lends)
     def _():

time: 35 us -> 31.9 us (0.911)
  the two profiles are of different devices: /device:TPU:66 before, /device:TPU:1 now
where the time goes in v3:
time: 31.9 us; the launch traced here: 31.8 us
  Pallas kernels  31.1 us (97%)
  between operations  0.64 us (2%)
    pallas_call x1, Pallas kernels, local(): pl.pallas_call(kernel, out_shape=(rows, rows), in_specs=[anywhere] * 10,...  28.6 us
    pallas_call x1, Pallas kernels, local(): pl.pallas_call(finish, out_shape=(jax.ShapeDtypeStruct((ROWS, 2, WIDE), F...  2.49 us

profile of v3, /device:TPU:1, one launch (start us, length us, event | category | flops | bytes accessed | tf_op | source)
XLA Modules:
  0.0 31.8 jit_solution(353251003553743446)
XLA Ops:
  0.6 28.6 %substep.1 = (f32[648,128]{1,0:T(8,128)}, f32[648,128]{1,0:T(8,128)}) custom-call(s32[288]{0:T(512)} %cut_in.1, f32[1152]{0:T(1024)} %constant.12.clone.geo_in, f32[9,2,2880]{2,1,0:T(2,128)} %bitcast.4, f32[9,2880]{1,0:T(8,128)} %thick.1, bf16[9,3,2880]{2,1,0:T(4,128)(2,1)} %bitcast.6, bf16[736,192]{1,0:T(8,128)(2,1)} %constant.13.clone.fore_in, ...), custom_call_target="tpu_custom_call" | custom-call | tf_op jit(solution)/shard_map/substep/pallas_call | solution.py:578
  29.3 2.5 %finish.1 = (f32[9,2,2880]{2,1,0:T(2,128)}, f32[9,2880]{1,0:T(8,128)}, bf16[9,3,2880]{2,1,0:T(4,128)(2,1)}) custom-call(f32[9,2,2880]{2,1,0:T(2,128)} %bitcast.5, f32[9,2880]{1,0:T(8,128)} %thick.1, f32[648,128]{1,0:T(8,128)} %get-tuple-element.8.steps, f32[648,128]{1,0:T(8,128)} %get-tuple-element.9.mass), custom_call_target="tpu_custom_call" | custom-call | tf_op jit(solution)/shard_map/finish/pallas_call | solution.py:606

commit v4 on v3

--- a/solution.py
+++ b/solution.py
@@ -130,10 +130,10 @@
 
 def kernel(
     cut_in, geo_in, winds_in, thick_in, mass_in, fore_in, twiddle_in, mix_in, unmix_in, back_in,
-    returned, mass,
-    wv, hv, qv, cells, to_east, to_west, from_west, from_east, tend, gathered, sent_back,
+    returned, mass_out,
+    wv, hv, qv, mv, mass, cells, to_east, to_west, from_west, from_east, tend, gathered, sent_back,
     fore, twiddle, mix, unmix, back, cut, geo,
-    in_sem, table_sem, halo_send, halo_recv, go_send, go_recv, back_send, back_recv,
+    in_sem, table_sem, mass_sem, halo_send, halo_recv, go_send, go_recv, back_send, back_recv,
 ):
     lat = lax.axis_index("lat")
     lon = lax.axis_index("lon")
@@ -142,7 +142,17 @@
     polar = jnp.logical_or(polar_south, polar_north)
     other = (lat + N_LAT // 2) % N_LAT
     other_polar = jnp.logical_or(other * ROWS < POLAR, (other + 1) * ROWS > NLAT - POLAR)
-    lends = jnp.logical_and(other_polar, lon < AWAY)
+    ring = N_LON // 2
+
+    def away_place(sector):
+        return (sector % ring + 2) % ring * 2 + sector // ring
+
+    def partner(i):
+        k = ring - 1 - i // 2
+        offset = (k + 1) // 2 * (2 * (k % 2) - 1)
+        return (lon // ring + i % 2) % 2 * ring + (lon % ring + offset + ring) % ring
+
+    lends = jnp.logical_and(other_polar, away_place(lon) < AWAY)
 
     east = (lat, (lon + 1) % N_LON)
     west = (lat, (lon + N_LON - 1) % N_LON)
@@ -156,17 +166,29 @@
     def greet(device):
         pl.semaphore_signal(barrier, inc=1, device_id=device, device_id_type=MESH)
 
-    for device in (east, west, south, north):
+    @pl.when(polar)
+    def _():
+        def meet(i, carry):
+            near = partner(i)
+
+            @pl.when(away_place(near) < AWAY)
+            def _():
+                greet((other, near))
+
+            @pl.when(near != lon)
+            def _():
+                greet((lat, near))
+
+            return carry
+
+        lax.fori_loop(0, N_LON, meet, 0)
+
+    @pl.when(lends)
+    def _():
+        lax.fori_loop(0, N_LON, lambda i, c: (greet((other, partner(i))), c)[1], 0)
+
+    for device in (south, north, east, west):
         greet(device)
-
-    @pl.when(polar)
-    def _():
-        lax.fori_loop(1, N_LON, lambda i, c: (greet((lat, (lon + i) % N_LON)), c)[1], 0)
-        lax.fori_loop(0, AWAY, lambda i, c: (greet((other, i)), c)[1], 0)
-
-    @pl.when(lends)
-    def _():
-        lax.fori_loop(0, N_LON, lambda i, c: (greet((other, i)), c)[1], 0)
 
     loads = [
         pltpu.make_async_copy(winds_in, wv, in_sem.at[0]),
@@ -281,12 +303,6 @@
         inner = slice(1, ROWS - 1)
         tend[at, :] = jnp.where(lane[inner] < TAIL, tend[at, :], value[inner])
 
-    def partner(i):
-        ring = N_LON // 2
-        k = ring - 1 - i // 2
-        offset = (k + 1) // 2 * (2 * (k % 2) - 1)
-        return (lon // ring + i % 2) % 2 * ring + (lon % ring + offset + ring) % ring
-
     def pair_of(i):
         return (2 * i + PAIRS - 4) % PAIRS
 
@@ -368,9 +384,9 @@
             def _():
                 go(pair_of(near), (lat, near)).start()
 
-            @pl.when(near < AWAY)
+            @pl.when(away_place(near) < AWAY)
             def _():
-                go(pair_of(OWN + near), (other, near)).start()
+                go(pair_of(OWN + away_place(near)), (other, near)).start()
 
             return carry
 
@@ -466,11 +482,11 @@
         for load in tables:
             load.wait()
         wait_for(gathered, N_LON, go_recv)
-        circle(pair_of(OWN + lon), other * ROWS)
+        circle(pair_of(OWN + away_place(lon)), other * ROWS)
 
         def away(i, carry):
             target = partner(i)
-            home(pair_of(OWN + lon), target, (other, target)).start()
+            home(pair_of(OWN + away_place(lon)), target, (other, target)).start()
             return carry
 
         lax.fori_loop(0, N_LON, away, 0)
@@ -511,6 +527,17 @@
 
     lax.fori_loop(0, ROWS, tracer, 0)
 
+    def narrow(j, carry):
+        for t in range(FULL + 1):
+            width = LANES if t < FULL else TAIL
+            value = mass[pl.ds(j * 3 * TILES + t, 3, stride=TILES), :]
+            mv[j, :, pl.ds(t * LANES, width)] = value[:, :width].astype(BF16)
+        return carry
+
+    lax.fori_loop(0, ROWS, narrow, 0)
+    keep_mass = pltpu.make_async_copy(mv, mass_out, mass_sem)
+    keep_mass.start()
+
     @pl.when(jnp.logical_not(lends))
     def _():
         for load in tables:
@@ -536,6 +563,7 @@
 
     halos[2].wait_send()
     halos[3].wait_send()
+    keep_mass.wait()
 
     @pl.when(polar)
     def _():
@@ -548,22 +576,39 @@
         wait_for(sent_back, N_LON, back_send)
 
 
-def finish(winds, thick, steps, mass, winds_out, thick_out, mass_out):
+def finish(winds, thick, steps, mass, winds_out, thick_out, mass_out, wv, hv, sv, mv, in_sem, out_sem):
+    def pair(n, source, held, target):
+        return pltpu.make_async_copy(source, held, in_sem.at[n]), pltpu.make_async_copy(held, target, out_sem.at[n])
+
+    mass_load, mass_store = pair(0, mass, mv, mass_out)
+    wind_load, wind_store = pair(1, winds, wv, winds_out)
+    thick_load, thick_store = pair(2, thick, hv, thick_out)
+    steps_load = pltpu.make_async_copy(steps, sv, in_sem.at[3])
+    for load in (steps_load, wind_load, thick_load, mass_load):
+        load.start()
+    steps_load.wait()
+    wind_load.wait()
+
     def one_row(j, carry):
-        start = j * 3 * TILES
         for t in range(FULL + 1):
             width = LANES if t < FULL else TAIL
             at = pl.ds(t * LANES, width)
-            step = steps[pl.ds(start + TILES + t, 2, stride=TILES), :]
-            winds_out[j, :, at] = winds[j, :, at] + TIME_STEP * step[:, :width]
-            mass_out[j, :, at] = mass[pl.ds(start + t, 3, stride=TILES), :][:, :width].astype(BF16)
+            step = sv[pl.ds((j * 3 + 1) * TILES + t, 2, stride=TILES), :]
+            wv[j, :, at] = wv[j, :, at] + TIME_STEP * step[:, :width]
         return carry
 
     lax.fori_loop(0, ROWS, one_row, 0)
+    wind_store.start()
+    mass_load.wait()
+    mass_store.start()
+    thick_load.wait()
     for t in range(FULL + 1):
         width = LANES if t < FULL else TAIL
         at = pl.ds(t * LANES, width)
-        thick_out[:, at] = thick[:, at] + TIME_STEP * steps[pl.ds(t, ROWS, stride=3 * TILES), :][:, :width]
+        hv[:, at] = hv[:, at] + TIME_STEP * sv[pl.ds(t, ROWS, stride=3 * TILES), :][:, :width]
+    thick_store.start()
+    for store in (wind_store, mass_store, thick_store):
+        store.wait()
 
 
 def local(winds, thickness, tracers, cutoff):
@@ -577,13 +622,15 @@
     tracers = jnp.transpose(tracers, (1, 0, 2))
     steps, mass = pl.pallas_call(
         kernel,
-        out_shape=(rows, rows),
+        out_shape=(rows, jax.ShapeDtypeStruct((ROWS, 3, WIDE), BF16)),
         in_specs=[anywhere] * 10,
-        out_specs=(whole, whole),
+        out_specs=(whole, anywhere),
         scratch_shapes=[
             pltpu.VMEM((ROWS, 2, WIDE), F32),
             pltpu.VMEM((ROWS, WIDE), F32),
             pltpu.VMEM((ROWS, 3, WIDE), BF16),
+            pltpu.VMEM((ROWS, 3, WIDE), BF16),
+            pltpu.VMEM((PAIRS * TILES, LANES), F32),
             pltpu.VMEM(((ROWS + 2) * SLOT, LANES), F32),
             side, side, side, side,
             pltpu.VMEM((PAIRS * TILES, LANES), F32),
@@ -596,7 +643,7 @@
             pltpu.VMEM(back.shape, BF16),
             pltpu.SMEM((NLAT,), jnp.int32),
             pltpu.SMEM((4 * NLAT,), F32),
-            dma((5,)), dma((5,)), dma((4,)), dma((4,)), dma, dma, dma, dma,
+            dma((5,)), dma((5,)), dma, dma((4,)), dma((4,)), dma, dma, dma, dma,
         ],
         compiler_params=pltpu.CompilerParams(
             collective_id=0, has_side_effects=True, vmem_limit_bytes=VMEM_MIB * 1024 * 1024
@@ -610,8 +657,16 @@
             jax.ShapeDtypeStruct((ROWS, WIDE), F32),
             jax.ShapeDtypeStruct((ROWS, 3, WIDE), BF16),
         ),
-        in_specs=[whole] * 4,
-        out_specs=(whole,) * 3,
+        in_specs=[anywhere] * 4,
+        out_specs=(anywhere,) * 3,
+        scratch_shapes=[
+            pltpu.VMEM((ROWS, 2, WIDE), F32),
+            pltpu.VMEM((ROWS, WIDE), F32),
+            pltpu.VMEM((PAIRS * TILES, LANES), F32),
+            pltpu.VMEM((ROWS, 3, WIDE), BF16),
+            dma((4,)), dma((3,)),
+        ],
+        compiler_params=pltpu.CompilerParams(vmem_limit_bytes=VMEM_MIB * 1024 * 1024),
         name="finish",
     )(winds, thickness, steps, mass)
     return jnp.transpose(new_winds, (1, 0, 2)), new_thickness, jnp.transpose(new_mass, (1, 0, 2))

time: 31.9 us -> 30.7 us (0.962)
  Pallas kernels: 31.1 us -> 29.9 us
    pallas_call x1, Pallas kernels: 28.6 us -> 27.8 us  [local(): pl.pallas_call(kernel, out_shape=(rows, jax.ShapeDtypeStruct((ROWS, 3, WI...]
    pallas_call x1, Pallas kernels: 2.49 us -> 2.11 us  [local(): pl.pallas_call(finish, out_shape=(jax.ShapeDtypeStruct((ROWS, 2, WIDE), F...]
where the time goes in v4:
time: 30.7 us; the launch traced here: 30.5 us
  Pallas kernels  29.9 us (97%)
  between operations  0.64 us (2%)
    pallas_call x1, Pallas kernels, local(): pl.pallas_call(kernel, out_shape=(rows, jax.ShapeDtypeStruct((ROWS, 3, WI...  27.8 us
    pallas_call x1, Pallas kernels, local(): pl.pallas_call(finish, out_shape=(jax.ShapeDtypeStruct((ROWS, 2, WIDE), F...  2.11 us

profile of v4, /device:TPU:1, one launch (start us, length us, event | category | flops | bytes accessed | tf_op | source)
XLA Modules:
  0.0 30.5 jit_solution(14276307261498281885)
XLA Ops:
  0.6 27.8 %substep.1 = (f32[648,128]{1,0:T(8,128)}, bf16[9,3,2880]{2,1,0:T(4,128)(2,1)}) custom-call(s32[288]{0:T(512)} %cut_in.1, f32[1152]{0:T(1024)} %constant.12.clone.geo_in, f32[9,2,2880]{2,1,0:T(2,128)} %bitcast.4, f32[9,2880]{1,0:T(8,128)} %thick.1, bf16[9,3,2880]{2,1,0:T(4,128)(2,1)} %bitcast.6, bf16[736,192]{1,0:T(8,128)(2,1)} %constant.13.clone.fore_in, ...), custom_call_target="tpu_custom_call" | custom-call | tf_op jit(solution)/shard_map/substep/pallas_call | solution.py:623
  28.4 2.1 %finish.1 = (f32[9,2,2880]{2,1,0:T(2,128)}, f32[9,2880]{1,0:T(8,128)}, bf16[9,3,2880]{2,1,0:T(4,128)(2,1)}) custom-call(f32[9,2,2880]{2,1,0:T(2,128)} %bitcast.5, f32[9,2880]{1,0:T(8,128)} %thick.1, f32[648,128]{1,0:T(8,128)} %get-tuple-element.8.steps, bf16[9,3,2880]{2,1,0:T(4,128)(2,1)} %get-tuple-element.9.mass), custom_call_target="tpu_custom_call" | custom-call | tf_op jit(solution)/shard_map/finish/pallas_call | solution.py:653

commit v5 on v4

--- a/solution.py
+++ b/solution.py
@@ -60,12 +60,6 @@
     return table.astype(np.float32).reshape(-1)
 
 
-def split_table(table):
-    high = table.astype(np.float32).astype(jnp.bfloat16)
-    low = (table - high.astype(np.float64)).astype(np.float32).astype(jnp.bfloat16)
-    return np.concatenate([high, low], axis=0)
-
-
 def filter_tables():
     turn = 2.0 * math.pi
     freq = np.arange(FREQ)
@@ -91,29 +85,12 @@
     mix = np.concatenate(
         [np.concatenate([cosine, -sine], axis=1), np.concatenate([sine, cosine], axis=1)], axis=0
     )
-    return split_table(fore), twiddle, split_table(mix), split_table(mix.T), split_table(back)
-
-
-def split(value):
-    high = value.astype(BF16)
-    low = (value - high.astype(F32)).astype(BF16)
-    return high, low
+    fore, mix, unmix, back = (a.astype(np.float32).astype(jnp.bfloat16) for a in (fore, mix, mix.T, back))
+    return fore, twiddle, mix, unmix, back
 
 
 def dot(a, b):
-    return jnp.dot(a, b, preferred_element_type=F32)
-
-
-def table_left(table, rows, value):
-    high, low = split(value)
-    first = table[pl.ds(0, rows), :]
-    return dot(first, high) + dot(first, low) + dot(table[pl.ds(rows, rows), :], high)
-
-
-def table_right(value, table, rows):
-    high, low = split(value)
-    first = table[pl.ds(0, rows), :]
-    return dot(high, first) + dot(low, first) + dot(high, table[pl.ds(rows, rows), :])
+    return jnp.dot(a.astype(BF16), b.astype(BF16), preferred_element_type=F32)
 
 
 def eastward(value):
@@ -133,7 +110,7 @@
     returned, mass_out,
     wv, hv, qv, mv, mass, cells, to_east, to_west, from_west, from_east, tend, gathered, sent_back,
     fore, twiddle, mix, unmix, back, cut, geo,
-    in_sem, table_sem, mass_sem, halo_send, halo_recv, go_send, go_recv, back_send, back_recv,
+    in_sem, table_sem, mass_sem, keep_sem, halo_send, halo_recv, go_send, go_recv, back_send, back_recv,
 ):
     lat = lax.axis_index("lat")
     lon = lax.axis_index("lon")
@@ -448,20 +425,20 @@
         complete(pair, lat_row)
         cutoff = cut[lat_row]
         data = jnp.concatenate([gathered[pl.ds(0, SIDE), :], gathered[pl.ds(SIDE, SIDE), :]], axis=1)
-        lines = table_left(fore, 2 * FREQ, data)
+        lines = dot(fore[...], data)
         real, imag = lines[:FREQ], lines[FREQ:]
         cosine, sine = twiddle[pl.ds(0, FREQ), :], twiddle[pl.ds(FREQ, FREQ), :]
         turned = jnp.concatenate([real * cosine + imag * sine, imag * cosine - real * sine], axis=1)
-        spectrum = table_right(turned, mix, 4 * LANES)
+        spectrum = dot(turned, mix[...])
         wave = lax.broadcasted_iota(jnp.int32, (FREQ, 2 * LANES), 0) + BASE * (
             lax.broadcasted_iota(jnp.int32, (FREQ, 2 * LANES), 1) % LANES // LEVELS
         )
         wave = jnp.minimum(wave, NLON - wave)
         spectrum = jnp.where(wave <= cutoff, spectrum, 0.0)
-        lines = table_right(spectrum, unmix, 2 * LANES)
+        lines = dot(spectrum, unmix[...])
         real, imag = lines[:, : 2 * LANES], lines[:, 2 * LANES :]
         turned = jnp.concatenate([real * cosine - imag * sine, real * sine + imag * cosine], axis=0)
-        result = table_left(back, SIDE, turned)
+        result = dot(back[...], turned)
         sent_back[pl.ds(0, SIDE), :] = result[:, :LANES]
         sent_back[pl.ds(SIDE, SIDE), :] = result[:, LANES:]
 
@@ -470,6 +447,9 @@
             block(sent_back, place(sector)), block(returned, pair), back_send, back_recv,
             device_id=device, device_id_type=MESH,
         )
+
+    def own_block():
+        return pltpu.make_async_copy(block(sent_back, place(lon)), block(returned, pair_of(lon)), keep_sem)
 
     def total(ref, blocks):
         return ref.at[pl.ds(0, blocks * BLOCK), :]
@@ -509,7 +489,8 @@
 
     @pl.when(jnp.logical_not(polar))
     def _():
-        lax.fori_loop(0, ROWS, lambda j, c: (tendency(j, returned, True), c)[1], 0)
+        lax.fori_loop(0, ROWS, lambda j, c: (tendency(j, tend, True), c)[1], 0)
+        pltpu.make_async_copy(tend, returned, keep_sem).start()
 
     def tracer(j, carry):
         inverse, sine, cos_north, cos_south = scalars(j)
@@ -558,8 +539,7 @@
             return carry
 
         lax.fori_loop(0, N_LON, own, 0)
-        at = pl.ds(pl.multiple_of(place(lon) * TILES, 8), BLOCK)
-        returned[pl.ds(pl.multiple_of(pair_of(lon) * TILES, 8), BLOCK), :] = sent_back[at, :]
+        own_block().start()
 
     halos[2].wait_send()
     halos[3].wait_send()
@@ -569,7 +549,12 @@
     def _():
         wait_for(tend, PAIRS - 1, go_send)
         wait_for(sent_back, N_LON - 1, back_send)
-        wait_for(returned, PAIRS - 1, back_recv)
+        own_block().wait()
+        wait_for(tend, PAIRS - 1, back_recv)
+
+    @pl.when(jnp.logical_not(polar))
+    def _():
+        pltpu.make_async_copy(tend, returned, keep_sem).wait()
 
     @pl.when(lends)
     def _():
@@ -614,7 +599,6 @@
 def local(winds, thickness, tracers, cutoff):
     fore, twiddle, mix, unmix, back = filter_tables()
     anywhere = pl.BlockSpec(memory_space=pl.ANY)
-    whole = pl.BlockSpec(memory_space=pltpu.VMEM)
     side = pltpu.VMEM((48, LANES), F32)
     dma = pltpu.SemaphoreType.DMA
     rows = jax.ShapeDtypeStruct((PAIRS * TILES, LANES), F32)
@@ -624,7 +608,7 @@
         kernel,
         out_shape=(rows, jax.ShapeDtypeStruct((ROWS, 3, WIDE), BF16)),
         in_specs=[anywhere] * 10,
-        out_specs=(whole, anywhere),
+        out_specs=(anywhere, anywhere),
         scratch_shapes=[
             pltpu.VMEM((ROWS, 2, WIDE), F32),
             pltpu.VMEM((ROWS, WIDE), F32),
@@ -643,7 +627,7 @@
             pltpu.VMEM(back.shape, BF16),
             pltpu.SMEM((NLAT,), jnp.int32),
             pltpu.SMEM((4 * NLAT,), F32),
-            dma((5,)), dma((5,)), dma, dma((4,)), dma((4,)), dma, dma, dma, dma,
+            dma((5,)), dma((5,)), dma, dma, dma((4,)), dma((4,)), dma, dma, dma, dma,
         ],
         compiler_params=pltpu.CompilerParams(
             collective_id=0, has_side_effects=True, vmem_limit_bytes=VMEM_MIB * 1024 * 1024

time: 30.7 us -> 29.5 us (0.961)
  Pallas kernels: 29.9 us -> 28.7 us
    pallas_call x1, Pallas kernels: 27.8 us -> 26.6 us  [local(): pl.pallas_call(kernel, out_shape=(rows, jax.ShapeDtypeStruct((ROWS, 3, WI...]
where the time goes in v5:
time: 29.5 us; the launch traced here: 29.3 us
  Pallas kernels  28.7 us (97%)
  between operations  0.64 us (2%)
    pallas_call x1, Pallas kernels, local(): pl.pallas_call(kernel, out_shape=(rows, jax.ShapeDtypeStruct((ROWS, 3, WI...  26.6 us
    pallas_call x1, Pallas kernels, local(): pl.pallas_call(finish, out_shape=(jax.ShapeDtypeStruct((ROWS, 2, WIDE), F...  2.11 us

profile of v5, /device:TPU:1, one launch (start us, length us, event | category | flops | bytes accessed | tf_op | source)
XLA Modules:
  0.0 29.3 jit_solution(16237301086825914185)
XLA Ops:
  0.6 26.6 %substep.1 = (f32[648,128]{1,0:T(8,128)}, bf16[9,3,2880]{2,1,0:T(4,128)(2,1)}) custom-call(s32[288]{0:T(512)} %cut_in.1, f32[1152]{0:T(1024)} %constant.12.clone.geo_in, f32[9,2,2880]{2,1,0:T(2,128)} %bitcast.4, f32[9,2880]{1,0:T(8,128)} %thick.1, bf16[9,3,2880]{2,1,0:T(4,128)(2,1)} %bitcast.6, bf16[368,192]{1,0:T(8,128)(2,1)} %constant.13.clone.fore_in, ...), custom_call_target="tpu_custom_call" | custom-call | tf_op jit(solution)/shard_map/substep/pallas_call | solution.py:607
  27.2 2.1 %finish.1 = (f32[9,2,2880]{2,1,0:T(2,128)}, f32[9,2880]{1,0:T(8,128)}, bf16[9,3,2880]{2,1,0:T(4,128)(2,1)}) custom-call(f32[9,2,2880]{2,1,0:T(2,128)} %bitcast.5, f32[9,2880]{1,0:T(8,128)} %thick.1, f32[648,128]{1,0:T(8,128)} %get-tuple-element.8.steps, bf16[9,3,2880]{2,1,0:T(4,128)(2,1)} %get-tuple-element.9.mass), custom_call_target="tpu_custom_call" | custom-call | tf_op jit(solution)/shard_map/finish/pallas_call | solution.py:637
